TPU v7x, 1024 devices: a whole 8x8x8 slice. The times are simulated.
1024 devices in a mesh: wide: 16 (over y, z_hi), narrow: 64 (over z_lo, x, core).
Axes of the slice: x: 8, y: 8, z: 8 (z_hi: 2, z_lo: 4; z = z_hi * 4 + z_lo), core: 2. Of those that a mesh axis runs over, the one named last changes fastest.
Arguments:
- tokens: bfloat16 [256, 14848], P('narrow', 'wide'), may hold values from -6 to 6
- cotangent: bfloat16 [256, 14848], P('narrow', 'wide'), may hold values from -6 to 6
- codes_up: bfloat16 [14848, 30720], P('wide', 'narrow'), may hold values from -6 to 6
- scales_up: float32 [14848, 320], P('wide', 'narrow'), may hold values from 0.0041033262 to 0.012309978
- codes_down: bfloat16 [30720, 14848], P('narrow', 'wide'), may hold values from -6 to 6
- scales_down: float32 [320, 14848], P('narrow', 'wide'), may hold values from 0.0028527216 to 0.008558165
- up_rows: float32 [14848], P('wide'), may hold values from 12.8 to 384
- up_columns: float32 [30720], P('narrow'), may hold values from 12.8 to 384
- down_rows: float32 [30720], P('narrow'), may hold values from 12.8 to 384
- down_columns: float32 [14848], P('wide'), may hold values from 12.8 to 384
Outputs:
- mlp_out: bfloat16 [256, 14848], P('narrow', 'wide')
- input_grad: bfloat16 [256, 14848], P('narrow', 'wide')
- step_up: bfloat16 [14848, 30720], P('wide', 'narrow')
- step_down: bfloat16 [30720, 14848], P('narrow', 'wide')
All inputs are finite; a program needn't handle non-finite values.
Results may differ from a plain program's by a relative error of at most 0.0068.
Values may be sent and summed in bfloat16 or wider, within the bound.
No kernel may reach another device: no remote copies, remote signals or barrier semaphores. Data moves between devices by JAX's collectives and lax.ppermute only.
A program may use at most 32 MiB of HBM per device.

v0:
```python
import jax
import jax.numpy as jnp
from jax import lax
from jax.sharding import PartitionSpec as P

D = 14848
FF = 30720
QB = 96


decay_rate = 0.9
square_eps = 1e-30


def gelu_value(value):
    return 0.5 * value * (1.0 + lax.erf(value * 0.7071067811865476))


def gelu_slope(value):
    return (
        0.5 * (1.0 + lax.erf(value * 0.7071067811865476))
        + value * jnp.exp(-0.5 * value * value) * 0.3989422804014327
    )


def contract_last(left, right):
    return lax.dot_general(
        left, right, (((1,), (1,)), ((), ())), preferred_element_type=jnp.float32
    )


def contract_first(left, right):
    return lax.dot_general(
        left, right, (((0,), (0,)), ((), ())), preferred_element_type=jnp.float32
    )


def on_device(
    tokens,
    cotangent,
    codes_up,
    scales_up,
    codes_down,
    scales_down,
    up_rows,
    up_columns,
    down_rows,
    down_columns,
):
    local_width = codes_up.shape[0]
    local_hidden = codes_up.shape[1]
    groups = local_hidden // QB
    w_up = (
        (codes_up.astype(jnp.float32).reshape(local_width, groups, QB) * scales_up[:, :, None])
        .reshape(local_width, local_hidden)
        .astype(jnp.bfloat16)
    )
    w_down = (
        (codes_down.astype(jnp.float32).reshape(groups, QB, local_width) * scales_down[:, None, :])
        .reshape(local_hidden, local_width)
        .astype(jnp.bfloat16)
    )
    tok_all, cot_all = (
        lax.all_gather(tokens, "narrow", axis=0, tiled=True),
        lax.all_gather(cotangent, "narrow", axis=0, tiled=True),
    )
    pre_part = jnp.dot(tok_all, w_up, preferred_element_type=jnp.float32)
    slope_part = contract_last(cot_all, w_down)
    pre, d_hidden = lax.psum((pre_part, slope_part), "wide")
    hidden = gelu_value(pre).astype(jnp.bfloat16)
    d_pre = (d_hidden * gelu_slope(pre)).astype(jnp.bfloat16)
    out_part = jnp.dot(hidden, w_down, preferred_element_type=jnp.float32)
    grad_part = contract_last(d_pre, w_up)
    out_sum, grad_sum = (
        lax.psum_scatter(out_part, "narrow", scatter_dimension=0, tiled=True),
        lax.psum_scatter(grad_part, "narrow", scatter_dimension=0, tiled=True),
    )
    g_up = contract_first(tok_all, d_pre)
    g_down = contract_first(hidden, cot_all)
    sq_up = g_up * g_up + square_eps
    sq_down = g_down * g_down + square_eps
    rowsq_up, colsq_down, state_total = lax.psum(
        (jnp.sum(sq_up, axis=1), jnp.sum(sq_down, axis=0), jnp.sum(down_rows)), "narrow"
    )
    row_new_up = decay_rate * up_rows + (1.0 - decay_rate) * rowsq_up / FF
    col_new_down = decay_rate * down_columns + (1.0 - decay_rate) * colsq_down / FF
    colsq_up, rowsq_down, row_total_up, square_total = lax.psum(
        (
            jnp.sum(sq_up, axis=0),
            jnp.sum(sq_down, axis=1),
            jnp.sum(row_new_up),
            jnp.sum(colsq_down),
        ),
        "wide",
    )
    col_new_up = decay_rate * up_columns + (1.0 - decay_rate) * colsq_up / D
    row_new_down = decay_rate * down_rows + (1.0 - decay_rate) * rowsq_down / D
    mean_up = row_total_up / D
    mean_down = (decay_rate * state_total + (1.0 - decay_rate) * square_total / D) / FF
    step_up = (
        g_up * lax.rsqrt(row_new_up / mean_up)[:, None] * lax.rsqrt(col_new_up)[None, :]
    ).astype(jnp.bfloat16)
    step_down = (
        g_down * lax.rsqrt(row_new_down / mean_down)[:, None] * lax.rsqrt(col_new_down)[None, :]
    ).astype(jnp.bfloat16)
    return (out_sum.astype(jnp.bfloat16), grad_sum.astype(jnp.bfloat16), step_up, step_down)


def solution(mesh):
    return jax.shard_map(
        on_device,
        mesh=mesh,
        in_specs=(
            P("narrow", "wide"),
            P("narrow", "wide"),
            P("wide", "narrow"),
            P("wide", "narrow"),
            P("narrow", "wide"),
            P("narrow", "wide"),
            P("wide"),
            P("narrow"),
            P("narrow"),
            P("wide"),
        ),
        out_specs=(
            P("narrow", "wide"),
            P("narrow", "wide"),
            P("wide", "narrow"),
            P("narrow", "wide"),
        ),
        check_vma=False,
    )
```

profile of v0, /device:TPU:16, one launch (start us, length us, event | category | flops | bytes accessed | tf_op | source)
XLA Modules:
  0.0 753.9 jit_solution(10018736823995634098)
XLA Ops:
  7.2 0.0 all-reduce.8.cloned.1.call-start
  7.2 1.7 copy.19
  8.9 0.0 copy-start.8
  8.9 86.1 %all-gather.1 = bf16[64,4,928]{2,1,0:T(4,128)(2,1)S(1)} all-gather(bf16[1,4,928]{2,1,0:T(4,128)(2,1)S(1)} %bitcast.27), channel_id=1, replica_groups=mesh['wide'=16,'narrow'=64] {'narrow'}, dimensions={0}, use_global_device_ids=true | all-gather | bytes 482560 | tf_op jit(solution)/shard_map/all_gather | solution.py:65
  95.0 1.0 reshape.23
  96.0 0.0 copy-done.3
  96.0 0.7 copy.18
  96.7 0.0 copy-done.8
  96.7 75.4 %all-gather = bf16[64,4,928]{2,1,0:T(4,128)(2,1)S(1)} all-gather(bf16[1,4,928]{2,1,0:T(4,128)(2,1)S(1)} %bitcast.28), channel_id=1, replica_groups=mesh['wide'=16,'narrow'=64] {'narrow'}, dimensions={0}, use_global_device_ids=true | all-gather | bytes 482560 | tf_op jit(solution)/shard_map/all_gather | solution.py:64
  172.1 0.2 reshape.21
  172.3 0.0 copy-start.5
  172.3 0.2 fusion
  172.6 2.3 convolution_bitcast_fusion
  174.9 0.2 fusion.1
  175.1 0.0 copy-start.9
  175.2 1.2 convolution_bitcast_fusion.1
  176.4 0.0 all-reduce.8.cloned.1.call-update
  176.4 0.6 reduce_sum.67
  177.0 1.3 dynamic-slice
  179.0 217.7 %all-reduce.8.cloned.1.call-done = (f32[256,480]{0,1:T(8,128)}, f32[256,480]{0,1:T(8,128)}) async-done(((f32[256,480]{0,1:T(8,128)}, f32[256,480]{0,1:T(8,128)}), (f32[256,480]{0,1:T(8,128)}, f32[256,480]{0,1:T(8,128)})) %all-reduce.8.cloned.1.call-update) | async-done | bytes 983056 | tf_op jit(solution)/shard_map/psum | solution.py:69
  396.7 1.4 fusion.12
  398.1 0.0 copy-start.1
  398.1 1.8 fusion.3
  399.9 0.5 fusion.16
  400.3 1.8 fusion.5
  402.1 0.5 fusion.15
  402.6 290.3 %all-reduce.9 = (bf16[256,928]{1,0:T(8,128)(2,1)}, bf16[256,928]{1,0:T(8,128)(2,1)}, f32[928]{0:T(1024)S(1)}, f32[928]{0:T(1024)S(1)}, f32[]{:T(128)}) all-reduce(f32[256,928]{1,0:T(8,128)S(1)} %fusion.15, f32[256,928]{1,0:T(8,128)S(1)} %fusion.16, ...), channel_id=2, replica_groups=mesh['wide'=16,'narrow'=64] {'narrow'}, use_global_device_ids=true, to_apply=%region_1.0.clone | all-reduce | flops 476993 | bytes 2865672
  692.9 0.6 add_rsqrt_fusion
  693.5 46.4 %all-reduce.3 = (f32[480]{0:T(512)S(1)}, f32[]{:T(128)}, f32[480]{0:T(512)S(1)}, f32[]{:T(128)}) all-reduce(f32[480]{0:T(512)S(1)} %get-tuple-element.7, f32[]{:T(128)} %get-tuple-element.25, f32[480]{0:T(512)S(1)} %get-tuple-element.4, f32[]{:T(128)} %get-tuple-element.20), channel_id=1, replica_groups=mesh['wide'=16,'narrow'=64] {'wide'}, use_global_device_ids=true, to_apply=%region_9.0 | all-reduce | flops 962 | bytes 7696 | tf_op jit(solution)/shard_map/psum | solution.py:87
  741.9 2.7 multiply_convert_fusion
  744.5 1.2 fusion.6
  745.7 1.3 dynamic-slice_convert_fusion
  (21 shorter events, 0.1 us)
Async XLA Ops:
  7.2 1.8 copy-start.7
  7.2 88.9 %copy-start.3 = (bf16[928,480]{1,0:T(8,128)(2,1)S(1)}, bf16[928,480]{1,0:T(8,128)(2,1)}, u32[]{:S(2)}) copy-start(bf16[928,480]{1,0:T(8,128)(2,1)} %param.12) | copy-start | bytes 2672644
  7.2 389.5 %all-reduce.8.cloned.1.call-start = ((), (), s32[]{:S(2)}) async-start(), calls=%async_computation | async-start | bytes 1966080 | tf_op jit(solution)/shard_map/psum | solution.py:69
  8.9 87.8 %copy-start.8 = (bf16[4,928]{1,0:T(4,128)(2,1)S(1)}, bf16[4,928]{1,0:T(4,128)(2,1)}, u32[]{:S(2)}) copy-start(bf16[4,928]{1,0:T(4,128)(2,1)} %param.10) | copy-start | bytes 22276
  96.0 76.3 %copy-start.4 = (f32[5,928]{1,0:T(8,128)S(1)}, f32[5,928]{1,0:T(8,128)}, u32[]{:S(2)}) copy-start(f32[5,928]{1,0:T(8,128)} %param.15) | copy-start | bytes 55684
  172.3 2.6 copy-start.5
  175.1 1.3 copy-start.9
  398.1 2.3 copy-start.1
  398.1 2.3 copy-start.2
  402.1 290.7 %copy-start.6 = (f32[928]{0:T(1024)S(1)}, f32[928]{0:T(1024)}, u32[]{:S(2)}) copy-start(f32[928]{0:T(1024)} %param.16) | copy-start | bytes 11140
  402.1 290.7 %copy-start.10 = (f32[928]{0:T(1024)S(1)}, f32[928]{0:T(1024)}, u32[]{:S(2)}) copy-start(f32[928]{0:T(1024)} %param.19) | copy-start | bytes 11140
  402.1 339.7 %copy-start.11 = (f32[480]{0:T(512)S(1)}, f32[480]{0:T(512)}, u32[]{:S(2)}) copy-start(f32[480]{0:T(512)} %param.17) | copy-start | bytes 5764
  692.9 51.7 %copy-start = (f32[480,928]{0,1:T(8,128)S(1)}, f32[480,928]{0,1:T(8,128)}, u32[]{:S(2)}) copy-start(f32[480,928]{0,1:T(8,128)} %get-tuple-element.21) | copy-start | bytes 5345284
Sparse Core Ops, SparseCore 0:
  176.5 220.1 all-reduce.7
where the time goes:
time: 754 us
  blocking collectives  498 us (66%)
  waiting for transfers between devices  218 us (29%)
  between operations  16.8 us (2%)
  matrix products  8.02 us (1%)
    unnamed x1, blocking collectives  290 us
    psum x1, waiting for transfers between devices, on_device(): pre, d_hidden = lax.psum((pre_part, slope_part), 'wide')  218 us
    all_gather x1, blocking collectives, on_device(): lax.all_gather(cotangent, 'narrow', axis=0, tiled=True)  86.1 us
    all_gather x1, blocking collectives, on_device(): lax.all_gather(tokens, 'narrow', axis=0, tiled=True)  75.4 us
    psum x1, blocking collectives, on_device(): lax.psum((jnp.sum(sq_up, axis=0), jnp.sum(sq_down, axis=1), jnp.sum(row_n...  46.4 us
  transfers between devices with their start and end apart: 1, of which 1 were waited for; matrix products, arithmetic and copies ran while one was open for 0% of the time, Pallas kernels for 0%

commit v1 on v0

--- a/solution.py
+++ b/solution.py
@@ -50,6 +50,21 @@
     local_width = codes_up.shape[0]
     local_hidden = codes_up.shape[1]
     groups = local_hidden // QB
+    own_tokens = tokens.shape[0]
+    wide = lax.axis_size("wide")
+    narrow = lax.axis_size("narrow")
+    chips = narrow // 2
+    pairs = [(i, i ^ 1) for i in range(narrow)]
+    same_core = [[2 * i + core for i in range(chips)] for core in range(2)]
+    packed = jnp.concatenate([tokens, cotangent], axis=0)
+    mine = lax.all_to_all(
+        jnp.broadcast_to(packed[None], (chips,) + packed.shape),
+        "narrow",
+        0,
+        0,
+        axis_index_groups=same_core,
+    )
+    other = lax.ppermute(mine, "narrow", pairs)
     w_up = (
         (codes_up.astype(jnp.float32).reshape(local_width, groups, QB) * scales_up[:, :, None])
         .reshape(local_width, local_hidden)
@@ -60,50 +75,92 @@
         .reshape(local_hidden, local_width)
         .astype(jnp.bfloat16)
     )
-    tok_all, cot_all = (
-        lax.all_gather(tokens, "narrow", axis=0, tiled=True),
-        lax.all_gather(cotangent, "narrow", axis=0, tiled=True),
+    both = jnp.concatenate([mine, other], axis=0)
+    tok_all = both[:, :own_tokens].reshape(-1, local_width)
+    cot_all = both[:, own_tokens:].reshape(-1, local_width)
+    pre_part = jnp.dot(tok_all, w_up, preferred_element_type=jnp.float32).astype(jnp.bfloat16)
+    slope_part = contract_last(cot_all, w_down).astype(jnp.bfloat16)
+    parts = jnp.stack(
+        [pre_part.reshape(wide, -1, local_hidden), slope_part.reshape(wide, -1, local_hidden)], axis=1
     )
-    pre_part = jnp.dot(tok_all, w_up, preferred_element_type=jnp.float32)
-    slope_part = contract_last(cot_all, w_down)
-    pre, d_hidden = lax.psum((pre_part, slope_part), "wide")
+    sums = jnp.sum(lax.all_to_all(parts, "wide", 0, 0).astype(jnp.float32), axis=0)
+    pre, d_hidden = sums[0], sums[1]
     hidden = gelu_value(pre).astype(jnp.bfloat16)
     d_pre = (d_hidden * gelu_slope(pre)).astype(jnp.bfloat16)
-    out_part = jnp.dot(hidden, w_down, preferred_element_type=jnp.float32)
-    grad_part = contract_last(d_pre, w_up)
-    out_sum, grad_sum = (
-        lax.psum_scatter(out_part, "narrow", scatter_dimension=0, tiled=True),
-        lax.psum_scatter(grad_part, "narrow", scatter_dimension=0, tiled=True),
-    )
+    acts = jnp.stack([hidden, d_pre], axis=0)
+    acts = lax.all_to_all(jnp.broadcast_to(acts[None], (wide,) + acts.shape), "wide", 0, 0)
+    hidden = acts[:, 0].reshape(-1, local_hidden)
+    d_pre = acts[:, 1].reshape(-1, local_hidden)
+
     g_up = contract_first(tok_all, d_pre)
     g_down = contract_first(hidden, cot_all)
     sq_up = g_up * g_up + square_eps
     sq_down = g_down * g_down + square_eps
-    rowsq_up, colsq_down, state_total = lax.psum(
-        (jnp.sum(sq_up, axis=1), jnp.sum(sq_down, axis=0), jnp.sum(down_rows)), "narrow"
+    over_wide = jnp.concatenate(
+        [jnp.sum(sq_up, axis=0), jnp.sum(sq_down, axis=1), jnp.sum(up_rows)[None]]
     )
+    over_wide = jnp.pad(over_wide, (0, -over_wide.shape[0] % 1024)).reshape(8, -1)
+    over_wide = lax.all_to_all(
+        jnp.broadcast_to(over_wide[None], (wide,) + over_wide.shape), "wide", 0, 0
+    )
+    over_wide = jnp.sum(over_wide, axis=0).reshape(-1)
+    colsq_up = over_wide[:local_hidden]
+    rowsq_down = over_wide[local_hidden : 2 * local_hidden]
+    up_rows_total = over_wide[2 * local_hidden]
+
+    stats = jnp.concatenate(
+        [
+            jnp.sum(sq_up, axis=1),
+            jnp.sum(sq_down, axis=0),
+            jnp.sum(colsq_up)[None],
+            jnp.sum(rowsq_down)[None],
+            jnp.sum(down_rows)[None],
+        ]
+    )
+    stats = stats + lax.ppermute(stats, "narrow", pairs)
+    totals = stats[2 * local_width :]
+    totals_high = totals.astype(jnp.bfloat16)
+    totals_low = (totals - totals_high.astype(jnp.float32)).astype(jnp.bfloat16)
+    stats = jnp.concatenate([stats[: 2 * local_width].astype(jnp.bfloat16), totals_high, totals_low])
+    spare = -(2 * own_tokens * local_width + stats.shape[0]) % (2 * own_tokens * 128)
+    stats = jnp.pad(stats, (0, spare)).reshape(2 * own_tokens, -1)
+
+    out_part = jnp.dot(hidden, w_down, preferred_element_type=jnp.float32)
+    grad_part = contract_last(d_pre, w_up)
+    mixed = jnp.concatenate(
+        [
+            out_part.reshape(2 * chips, own_tokens, local_width),
+            grad_part.reshape(2 * chips, own_tokens, local_width),
+        ],
+        axis=1,
+    )
+    from_pair = lax.ppermute(mixed[chips:].astype(jnp.bfloat16), "narrow", pairs)
+    mixed = (mixed[:chips] + from_pair.astype(jnp.float32)).astype(jnp.bfloat16)
+    mixed = jnp.concatenate(
+        [mixed, jnp.broadcast_to(stats[None], (chips,) + stats.shape)], axis=2
+    )
+    mixed = lax.all_to_all(mixed, "narrow", 0, 0, axis_index_groups=same_core)
+    mixed = jnp.sum(mixed.astype(jnp.float32), axis=0)
+    mlp_out = mixed[:own_tokens, :local_width].astype(jnp.bfloat16)
+    input_grad = mixed[own_tokens:, :local_width].astype(jnp.bfloat16)
+    stats = mixed[:, local_width:].reshape(-1)
+    rowsq_up = stats[:local_width]
+    colsq_down = stats[local_width : 2 * local_width]
+    totals = stats[2 * local_width : 2 * local_width + 3] + stats[2 * local_width + 3 : 2 * local_width + 6]
+
     row_new_up = decay_rate * up_rows + (1.0 - decay_rate) * rowsq_up / FF
-    col_new_down = decay_rate * down_columns + (1.0 - decay_rate) * colsq_down / FF
-    colsq_up, rowsq_down, row_total_up, square_total = lax.psum(
-        (
-            jnp.sum(sq_up, axis=0),
-            jnp.sum(sq_down, axis=1),
-            jnp.sum(row_new_up),
-            jnp.sum(colsq_down),
-        ),
-        "wide",
-    )
     col_new_up = decay_rate * up_columns + (1.0 - decay_rate) * colsq_up / D
     row_new_down = decay_rate * down_rows + (1.0 - decay_rate) * rowsq_down / D
-    mean_up = row_total_up / D
-    mean_down = (decay_rate * state_total + (1.0 - decay_rate) * square_total / D) / FF
+    col_new_down = decay_rate * down_columns + (1.0 - decay_rate) * colsq_down / FF
+    mean_up = (decay_rate * up_rows_total + (1.0 - decay_rate) * totals[0] / FF) / D
+    mean_down = (decay_rate * totals[2] + (1.0 - decay_rate) * totals[1] / D) / FF
     step_up = (
         g_up * lax.rsqrt(row_new_up / mean_up)[:, None] * lax.rsqrt(col_new_up)[None, :]
     ).astype(jnp.bfloat16)
     step_down = (
         g_down * lax.rsqrt(row_new_down / mean_down)[:, None] * lax.rsqrt(col_new_down)[None, :]
     ).astype(jnp.bfloat16)
-    return (out_sum.astype(jnp.bfloat16), grad_sum.astype(jnp.bfloat16), step_up, step_down)
+    return (mlp_out, input_grad, step_up, step_down)
 
 
 def solution(mesh):

time: 754 us -> 186 us (0.25)
  the two profiles are of different devices: /device:TPU:16 before, /device:TPU:2 now
where the time goes in v1:
time: 186 us; the launch traced here: 185 us
  blocking collectives  72.3 us (39%)
  waiting for transfers between devices  52.7 us (28%)
  starting transfers between devices  22.7 us (12%)
  local copies, waits for them, and re-layouts  17.7 us (10%)
  other arithmetic  9.7 us (5%)
  matrix products  5.95 us (3%)
  between operations  3.58 us (2%)
    all_to_all x1, blocking collectives, on_device(): lax.all_to_all(parts, 'wide', 0, 0).astype(jnp.float32)  39.2 us
    all_to_all x1, blocking collectives, on_device(): lax.all_to_all(jnp.broadcast_to(packed[None], (chips,) + packed.shape), '...  33.1 us
    all_to_all x1, waiting for transfers between devices, on_device(): lax.all_to_all(jnp.broadcast_to(acts[None], (wide,) + acts.shape), 'wide'...  19.9 us
    all_to_all x1, waiting for transfers between devices, on_device(): mixed = lax.all_to_all(mixed, 'narrow', 0, 0, axis_index_groups=same_core)  19.3 us
    all_to_all x1, waiting for transfers between devices, on_device(): lax.all_to_all(jnp.broadcast_to(over_wide[None], (wide,) + over_wide.shap...  12.3 us
    all_to_all x1, starting transfers between devices, on_device(): lax.all_to_all(jnp.broadcast_to(acts[None], (wide,) + acts.shape), 'wide'...  6.57 us
    all_to_all x1, starting transfers between devices, on_device(): lax.all_to_all(jnp.broadcast_to(over_wide[None], (wide,) + over_wide.shap...  5.27 us
    all_to_all x1, starting transfers between devices, on_device(): mixed = lax.all_to_all(mixed, 'narrow', 0, 0, axis_index_groups=same_core)  4.86 us
  transfers between devices with their start and end apart: 6, of which 4 were waited for; matrix products, arithmetic and copies ran while one was open for 7% of the time, Pallas kernels for 0%

profile of v1, /device:TPU:2, one launch (start us, length us, event | category | flops | bytes accessed | tf_op | source)
XLA Modules:
  0.0 184.7 jit_solution(15690525546052351020)
XLA Ops:
  0.7 0.9 pad_maximum_fusion.4
  1.6 33.1 %all_to_all.25 = bf16[32,8,928]{2,1,0:T(8,128)(2,1)} all-to-all(bf16[32,8,928]{2,1,0:T(8,128)(2,1)S(1)} %broadcast_in_dim.20), channel_id=1, replica_groups={{0,2,4,6,8,10,12,14,16,18,20,22,24,26,28,30,32,34,36,38,40,42,44,46,48,..., dimensions={0} | all-to-all | bytes 950272 | tf_op jit(solution)/shard_map/all_to_all | solution.py:60
  34.6 2.0 %collective-permute-start = (bf16[32,8,928]{2,1,0:T(8,128)(2,1)}, bf16[32,8,928]{2,1,0:T(8,128)(2,1)}, u32[]{:S(2)}, u32[]{:S(2)}) collective-permute-start(bf16[32,8,928]{2,1,0:T(8,128)(2,1)} %all_to_all.25), channel_id=1, source_target_pairs={{0,1},{1,0},{2,3},{3,2},{4,5},{5,4},{6,7},{7,6},{8,9},{9,8},{10,11... | collective-permute-start | bytes 1425416 | tf_op jit(solution)/shard_map/ppermute | solution.py:67
  38.6 1.1 constant_dynamic-update-slice_fusion.1
  39.7 1.1 constant_dynamic-update-slice_fusion
  40.8 1.1 fusion.28
  42.8 1.3 reshape.56
  44.1 1.1 convolution_convert_fusion.1
  45.2 1.8 copy.35
  47.0 1.0 pad_maximum_fusion.2
  48.1 39.2 %all_to_all.26 = bf16[16,2,16,480]{3,2,1,0:T(8,128)(2,1)S(1)} all-to-all(bf16[16,2,16,480]{3,2,1,0:T(8,128)(2,1)S(1)} %copy.38), channel_id=1, replica_groups=mesh['wide'=16,'narrow'=64] {'wide'}, dimensions={0} | all-to-all | bytes 983040 | tf_op jit(solution)/shard_map/all_to_all | solution.py:86
  87.4 0.9 broadcast_in_dim.21
  88.3 6.6 %all-to-all-start.2 = ((bf16[16,2,16,480]{3,2,1,0:T(8,128)(2,1)}), bf16[16,2,16,480]{3,2,1,0:T(8,128)(2,1)S(1)}, u32[]{:S(2)}, u32[]{:S(2)}) async-start(bf16[16,2,16,480]{3,2,1,0:T(8,128)(2,1)} %broadcast_in_dim.21), calls=%async_computation.2 | async-start | bytes 1048576 | tf_op jit(solution)/shard_map/all_to_all | solution.py:91
  95.5 19.9 %all-to-all-done.2 = bf16[16,2,16,480]{3,2,1,0:T(8,128)(2,1)S(1)} async-done(((bf16[16,2,16,480]{3,2,1,0:T(8,128)(2,1)}), bf16[16,2,16,480]{3,2,1,0:T(8,128)(2,1)S(1)}, u32[]{:S(2)}, u32[]{:S(2)}) %all-to-all-start.2) | async-done | bytes 491552 | tf_op jit(solution)/shard_map/all_to_all | solution.py:91
  115.4 0.7 fusion.29
  116.1 0.7 copy-done.5
  117.3 1.0 dot_general.26
  118.9 2.1 %collective-permute-start.1 = (bf16[32,8,928]{2,0,1:T(8,128)(2,1)S(1)}, bf16[32,8,928]{2,0,1:T(8,128)(2,1)S(1)}, u32[]{:S(2)}, u32[]{:S(2)}) collective-permute-start(bf16[32,8,928]{2,0,1:T(8,128)(2,1)S(1)} %fusion.9), channel_id=1, source_target_pairs={{0,1},{1,0},{2,3},{3,2},{4,5},{5,4},{6,7},{7,6},{8,9},{9,8},{10,11... | collective-permute-start | bytes 1425416 | tf_op jit(solution)/shard_map/ppermute | solution.py:137
  121.0 1.7 fusion.2
  122.7 1.8 fusion.4
  124.5 0.7 fusion.27
  125.9 5.3 %all-to-all-start.3 = ((f32[16,8,128]{2,1,0:T(8,128)}), f32[16,8,128]{2,1,0:T(8,128)S(1)}, u32[]{:S(2)}, u32[]{:S(2)}) async-start(f32[16,8,128]{2,1,0:T(8,128)} %broadcast_in_dim.48), calls=%async_computation.3 | async-start | bytes 131072 | tf_op jit(solution)/shard_map/all_to_all | solution.py:103
  131.7 12.3 %all-to-all-done.3 = f32[16,8,128]{2,1,0:T(8,128)S(1)} async-done(((f32[16,8,128]{2,1,0:T(8,128)}), f32[16,8,128]{2,1,0:T(8,128)S(1)}, u32[]{:S(2)}, u32[]{:S(2)}) %all-to-all-start.3) | async-done | bytes 65568 | tf_op jit(solution)/shard_map/all_to_all | solution.py:103
  144.1 0.7 slice_reduce_fusion
  144.8 2.0 %concatenate.25 = f32[1859]{0:T(1024)S(1)} concatenate(f32[928]{0:T(1024)S(1)} %get-tuple-element.5, f32[928]{0:T(1024)S(1)} %get-tuple-element.7, f32[1]{0:T(128)} %bitcast.11, f32[1]{0:T(128)} %bitcast.12, f32[1]{0:T(128)} %bitcast.13), dimensions={0} | concatenate | bytes 14872 | tf_op jit(solution)/shard_map/concatenate | solution.py:111
  146.8 1.9 %collective-permute-start.2 = (f32[1859]{0:T(1024)S(1)}, f32[1859]{0:T(1024)S(1)}, u32[]{:S(2)}, u32[]{:S(2)}) collective-permute-start(f32[1859]{0:T(1024)S(1)} %concatenate.25), channel_id=1, source_target_pairs={{0,1},{1,0},{2,3},{3,2},{4,5},{5,4},{6,7},{7,6},{8,9},{9,8},{10,11... | collective-permute-start | bytes 22316 | tf_op jit(solution)/shard_map/ppermute | solution.py:120
  148.7 1.1 collective-permute-done.2
  150.6 1.2 copy.43
  151.8 4.9 %all-to-all-start.4 = ((bf16[32,8,1280]{2,1,0:T(8,128)(2,1)}), bf16[32,8,1280]{2,1,0:T(8,128)(2,1)S(1)}, u32[]{:S(2)}, u32[]{:S(2)}) async-start(bf16[32,8,1280]{2,1,0:T(8,128)(2,1)} %copy.43), calls=%async_computation.4 | async-start | bytes 1310720 | tf_op jit(solution)/shard_map/all_to_all | solution.py:142
  157.9 19.3 %all-to-all-done.4 = bf16[32,8,1280]{2,1,0:T(8,128)(2,1)S(1)} async-done(((bf16[32,8,1280]{2,1,0:T(8,128)(2,1)}), bf16[32,8,1280]{2,1,0:T(8,128)(2,1)S(1)}, u32[]{:S(2)}, u32[]{:S(2)}) %all-to-all-start.4) | async-done | bytes 655392 | tf_op jit(solution)/shard_map/all_to_all | solution.py:142
  180.8 2.7 %multiply_convert_fusion.1 = bf16[928,480]{1,0:T(8,128)(2,1)} fusion(f32[928,480]{1,0:T(8,128)} %get-tuple-element.25, f32[480]{0:T(512)S(1)} %get-tuple-element.21, f32[928]{0:T(1024)S(1)} %get-tuple-element.19), kind=kLoop, calls=%fused_computation.7 | loop fusion | flops 1336320 | bytes 2678272 | tf_op jit(solution)/shard_map/convert_element_type | solution.py:159
  183.5 1.2 multiply_convert_fusion
  (73 shorter events, 8.7 us)
Async XLA Ops:
  0.6 36.1 %copy-start.8 = (bf16[928,480]{1,0:T(8,128)(2,1)S(1)}, bf16[928,480]{1,0:T(8,128)(2,1)}, u32[]{:S(2)}) copy-start(bf16[928,480]{1,0:T(8,128)(2,1)} %param.12) | copy-start | bytes 2672644
  0.6 36.7 %copy-start.9 = (bf16[480,928]{0,1:T(8,128)(2,1)S(1)}, bf16[480,928]{0,1:T(8,128)(2,1)}, u32[]{:S(2)}) copy-start(bf16[480,928]{0,1:T(8,128)(2,1)} %param.14) | copy-start | bytes 2672644
  34.6 3.4 %copy-start.10 = (f32[928,5]{0,1:T(8,128)S(1)}, f32[928,5]{0,1:T(8,128)}, u32[]{:S(2)}) copy-start(f32[928,5]{0,1:T(8,128)} %param.13) | copy-start | bytes 55684
  34.6 5.0 %collective-permute-start = (bf16[32,8,928]{2,1,0:T(8,128)(2,1)}, bf16[32,8,928]{2,1,0:T(8,128)(2,1)}, u32[]{:S(2)}, u32[]{:S(2)}) collective-permute-start(bf16[32,8,928]{2,1,0:T(8,128)(2,1)} %all_to_all.25), channel_id=1, source_target_pairs={{0,1},{1,0},{2,3},{3,2},{4,5},{5,4},{6,7},{7,6},{8,9},{9,8},{10,11... | collective-permute-start | bytes 1425416 | tf_op jit(solution)/shard_map/ppermute | solution.py:67
  37.4 0.9 copy-start.11
  42.1 3.1 %copy-start = (bf16[256,928]{1,0:T(8,128)(2,1)}, bf16[256,928]{1,0:T(8,128)(2,1)S(1)}, u32[]{:S(2)}) copy-start(bf16[256,928]{1,0:T(8,128)(2,1)S(1)} %reshape.57) | copy-start | bytes 1425412
  44.0 4.0 %copy-start.2 = (bf16[256,928]{1,0:T(8,128)(2,1)}, bf16[256,928]{1,0:T(8,128)(2,1)S(1)}, u32[]{:S(2)}) copy-start(bf16[256,928]{1,0:T(8,128)(2,1)S(1)} %reshape.56) | copy-start | bytes 1425412
  48.1 46.8 %copy-start.12 = (f32[928]{0:T(1024)S(1)}, f32[928]{0:T(1024)}, u32[]{:S(2)}) copy-start(f32[928]{0:T(1024)} %param.16) | copy-start | bytes 11140
  88.3 27.1 %all-to-all-start.2 = ((bf16[16,2,16,480]{3,2,1,0:T(8,128)(2,1)}), bf16[16,2,16,480]{3,2,1,0:T(8,128)(2,1)S(1)}, u32[]{:S(2)}, u32[]{:S(2)}) async-start(bf16[16,2,16,480]{3,2,1,0:T(8,128)(2,1)} %broadcast_in_dim.21), calls=%async_computation.2 | async-start | bytes 1048576 | tf_op jit(solution)/shard_map/all_to_all | solution.py:91
  116.1 0.7 copy-start.5
  118.4 2.6 %copy-start.3 = (bf16[256,928]{1,0:T(8,128)(2,1)S(1)}, bf16[256,928]{1,0:T(8,128)(2,1)}, u32[]{:S(2)}) copy-start(bf16[256,928]{1,0:T(8,128)(2,1)} %copy-done.2) | copy-start | bytes 1425412
  118.4 2.6 %copy-start.7 = (bf16[16,1,16,480]{3,2,1,0:T(8,128)(2,1)S(1)}, bf16[16,1,16,480]{3,2,1,0:T(8,128)(2,1)}, u32[]{:S(2)}) copy-start(bf16[16,1,16,480]{3,2,1,0:T(8,128)(2,1)} %get-tuple-element.13) | copy-start | bytes 737284
  118.9 3.8 %copy-start.1 = (bf16[256,928]{1,0:T(8,128)(2,1)S(1)}, bf16[256,928]{1,0:T(8,128)(2,1)}, u32[]{:S(2)}) copy-start(bf16[256,928]{1,0:T(8,128)(2,1)} %copy-done) | copy-start | bytes 1425412
  118.9 3.8 %copy-start.6 = (bf16[16,1,16,480]{3,2,1,0:T(8,128)(2,1)S(1)}, bf16[16,1,16,480]{3,2,1,0:T(8,128)(2,1)}, u32[]{:S(2)}) copy-start(bf16[16,1,16,480]{3,2,1,0:T(8,128)(2,1)} %copy-done.5) | copy-start | bytes 737284
  118.9 31.3 %collective-permute-start.1 = (bf16[32,8,928]{2,0,1:T(8,128)(2,1)S(1)}, bf16[32,8,928]{2,0,1:T(8,128)(2,1)S(1)}, u32[]{:S(2)}, u32[]{:S(2)}) collective-permute-start(bf16[32,8,928]{2,0,1:T(8,128)(2,1)S(1)} %fusion.9), channel_id=1, source_target_pairs={{0,1},{1,0},{2,3},{3,2},{4,5},{5,4},{6,7},{7,6},{8,9},{9,8},{10,11... | collective-permute-start | bytes 1425416 | tf_op jit(solution)/shard_map/ppermute | solution.py:137
  122.7 8.4 %copy-start.13 = (f32[480]{0:T(512)S(1)}, f32[480]{0:T(512)}, u32[]{:S(2)}) copy-start(f32[480]{0:T(512)} %param.18) | copy-start | bytes 5764
  125.9 18.2 %all-to-all-start.3 = ((f32[16,8,128]{2,1,0:T(8,128)}), f32[16,8,128]{2,1,0:T(8,128)S(1)}, u32[]{:S(2)}, u32[]{:S(2)}) async-start(f32[16,8,128]{2,1,0:T(8,128)} %broadcast_in_dim.48), calls=%async_computation.3 | async-start | bytes 131072 | tf_op jit(solution)/shard_map/all_to_all | solution.py:103
  146.8 3.1 %collective-permute-start.2 = (f32[1859]{0:T(1024)S(1)}, f32[1859]{0:T(1024)S(1)}, u32[]{:S(2)}, u32[]{:S(2)}) collective-permute-start(f32[1859]{0:T(1024)S(1)} %concatenate.25), channel_id=1, source_target_pairs={{0,1},{1,0},{2,3},{3,2},{4,5},{5,4},{6,7},{7,6},{8,9},{9,8},{10,11... | collective-permute-start | bytes 22316 | tf_op jit(solution)/shard_map/ppermute | solution.py:120
  150.5 30.1 %copy-start.14 = (f32[928]{0:T(1024)S(1)}, f32[928]{0:T(1024)}, u32[]{:S(2)}) copy-start(f32[928]{0:T(1024)} %param.19) | copy-start | bytes 11140
  150.5 30.2 %copy-start.15 = (f32[480]{0:T(512)S(1)}, f32[480]{0:T(512)}, u32[]{:S(2)}) copy-start(f32[480]{0:T(512)} %param.17) | copy-start | bytes 5764
  151.8 25.4 %all-to-all-start.4 = ((bf16[32,8,1280]{2,1,0:T(8,128)(2,1)}), bf16[32,8,1280]{2,1,0:T(8,128)(2,1)S(1)}, u32[]{:S(2)}, u32[]{:S(2)}) async-start(bf16[32,8,1280]{2,1,0:T(8,128)(2,1)} %copy.43), calls=%async_computation.4 | async-start | bytes 1310720 | tf_op jit(solution)/shard_map/all_to_all | solution.py:142
  156.6 26.9 %copy-start.4 = (f32[480,928]{0,1:T(8,128)S(1)}, f32[480,928]{0,1:T(8,128)}, u32[]{:S(2)}) copy-start(f32[480,928]{0,1:T(8,128)} %get-tuple-element.26) | copy-start | bytes 5345284

commit v2 on v0

v2 whole, which is shorter than its diff:
```python
import functools

import jax
import jax.numpy as jnp
from jax import lax
from jax.experimental import pallas as pl
from jax.experimental.pallas import tpu as pltpu
from jax.sharding import PartitionSpec as P

D = 14848
FF = 30720
QB = 96

decay_rate = 0.9
square_eps = 1e-30

bf16 = jnp.bfloat16
f32 = jnp.float32

WIDTH = 1024
UNITS = 512
GRAM = 256
SLOPE = UNITS + GRAM
LANES = SLOPE + UNITS
DIGITS = 6
DIGIT_UNIT = 8.0
STATS = 256
SPARE = 160


def gelu_value(value):
    return 0.5 * value * (1.0 + lax.erf(value * 0.7071067811865476))


def gelu_slope(value):
    return (
        0.5 * (1.0 + lax.erf(value * 0.7071067811865476))
        + value * jnp.exp(-0.5 * value * value) * 0.3989422804014327
    )


def mxu(left, right, left_dim=1, right_dim=0):
    return lax.dot_general(
        left, right, (((left_dim,), (right_dim,)), ((), ())), preferred_element_type=f32
    )


def iota(shape, dim):
    return lax.broadcasted_iota(jnp.int32, shape, dim)


def whole_call(kernel, outs, name):
    spec = pl.BlockSpec(memory_space=pltpu.VMEM)
    return lambda *args: pl.pallas_call(
        kernel,
        out_shape=[jax.ShapeDtypeStruct(shape, dtype) for shape, dtype in outs],
        in_specs=[spec] * len(args),
        out_specs=[spec] * len(outs),
        compiler_params=pltpu.CompilerParams(vmem_limit_bytes=24 * 1024 * 1024),
        name=name,
    )(*args)


def weights_kernel(codes_up, scales_up, codes_down, scales_down, w_up, w_down):
    width, units = codes_up.shape
    w_up[...] = jnp.zeros_like(w_up)
    w_down[...] = jnp.zeros_like(w_down)
    lane = iota((width, units), 1)
    scales = scales_up[:, 0:1]
    for group in range(1, units // QB):
        scales = jnp.where(lane >= group * QB, scales_up[:, group : group + 1], scales)
    w_up[:width, :units] = (codes_up[...].astype(f32) * scales).astype(bf16)
    for group in range(units // QB):
        rows = slice(group * QB, (group + 1) * QB)
        w_down[rows, :width] = (
            codes_down[rows, :].astype(f32) * scales_down[group : group + 1, :]
        ).astype(bf16)


def apart(count, own):
    half = count // 2
    row, column = iota((count, count), 0), iota((count, count), 1)
    second = (row >= half).astype(jnp.int32)
    token = row - second * half
    source = (token // own) * (2 * own) + second * own + token % own
    return (column == source).astype(f32).astype(bf16)


def partial_kernel(own, mine, other, w_up, w_down, up_rows, tok, cot, parts):
    count, width = mine.shape
    half = count // 2
    split = apart(count, own)
    for place, ref in ((0, mine), (half, other)):
        rows = mxu(split, ref[...]).astype(bf16)
        tok[place : place + half, :width] = rows[:half]
        cot[place : place + half, :width] = rows[half:]
    tok[:, width:] = jnp.zeros((count, WIDTH - width), bf16)
    cot[:, width:] = jnp.zeros((count, WIDTH - width), bf16)
    tokens, cotangents = tok[...], cot[...]
    parts[:, :UNITS] = mxu(tokens, w_up[...]).astype(bf16)
    row, column = iota((count, count), 0), iota((count, count), 1)
    gram_tok = mxu(tokens, tokens, 1, 1)
    gram_cot = mxu(cotangents, cotangents, 1, 1)
    parts[:, UNITS:SLOPE] = jnp.where(row >= column, gram_tok, gram_cot).astype(bf16)
    diagonal = jnp.sum(jnp.where(row == column, gram_cot, 0.0), axis=1, keepdims=True)
    slope = mxu(cotangents, w_down[...], 1, 1)
    units = UNITS - 32
    lane = iota((count, UNITS), 1)
    slope = jnp.where(lane == units, diagonal, slope)
    rest = jnp.floor(jnp.sum(up_rows[...], axis=1, keepdims=True) * DIGIT_UNIT + 0.5)
    for digit in range(DIGITS):
        shorter = jnp.floor(rest * (1.0 / 16.0))
        slope = jnp.where(lane == units + 1 + digit, rest - 16.0 * shorter, slope)
        rest = shorter
    parts[:, SLOPE:] = slope.astype(bf16)


def mix_kernel(local_hidden, acts, tok, cot, w_up, w_down, down_rows, send, keep, stats, squares):
    count = acts.shape[0]
    half = count // 2
    lane = iota((count, UNITS), 1)
    hidden = acts[:, :UNITS]
    d_wide = acts[:, SLOPE:].astype(f32)
    diagonal = 2.0 * d_wide[:, local_hidden : local_hidden + 1]
    d_wide = jnp.where(lane < local_hidden, d_wide, 0.0)
    d_pre = d_wide.astype(bf16)
    out = mxu(hidden, w_down[...])
    keep[:half, :] = out[:half]
    send[:half, :] = out[half:].astype(bf16)
    grad = mxu(d_pre, w_up[...], 1, 1)
    keep[half:, :] = grad[:half]
    send[half:count, :] = grad[half:].astype(bf16)
    row, column = iota((count, count), 0), iota((count, count), 1)
    gram = acts[:, UNITS:SLOPE].astype(f32)
    lower = jnp.where(row > column, 2.0 * gram, jnp.where(row == column, gram, 0.0)).astype(bf16)
    upper = jnp.where(row < column, 2.0 * gram, 0.0).astype(bf16)
    hidden_wide = hidden.astype(f32)
    colsq_up = jnp.sum(d_wide * mxu(lower, d_pre), axis=0, keepdims=True)
    rowsq_down = jnp.sum(
        hidden_wide * (mxu(upper, hidden) + diagonal * hidden_wide), axis=0, keepdims=True
    )
    real = iota((1, UNITS), 1) < local_hidden
    colsq_up = jnp.where(real, jnp.maximum(colsq_up, 0.0) + D * square_eps, 0.0)
    rowsq_down = jnp.where(real, jnp.maximum(rowsq_down, 0.0) + D * square_eps, 0.0)
    squares[0:1, :] = colsq_up
    squares[1:2, :] = rowsq_down
    totals = [
        jnp.sum(colsq_up, axis=1, keepdims=True),
        jnp.sum(rowsq_down, axis=1, keepdims=True),
        jnp.sum(down_rows[...], axis=1, keepdims=True),
    ]
    g_up = mxu(d_pre, tok[...], 0, 0)
    rowsq_up = jnp.sum(g_up * g_up, axis=0, keepdims=True) + local_hidden * square_eps
    g_down = mxu(hidden, cot[...], 0, 0)
    colsq_down = jnp.sum(g_down * g_down, axis=0, keepdims=True) + local_hidden * square_eps
    spare = iota((1, STATS), 1)
    for place, sums in ((0, rowsq_up), (4, colsq_down)):
        for part in range(4):
            piece = sums[:, part * STATS : (part + 1) * STATS]
            if part == 3:
                piece = jnp.where(spare < SPARE, piece, 0.0)
                for index, total in enumerate(totals):
                    piece = jnp.where(spare == SPARE + index, total, piece)
            stats[place + part : place + part + 1, :] = piece
    block = stats[...]
    high = block.astype(bf16).astype(f32)
    send[count:, :] = jnp.zeros((16, WIDTH), bf16)
    send[count:, :STATS] = jnp.concatenate([high, block - high], axis=0).astype(bf16)


def pair_kernel(own, keep, got, stats, mixed):
    count = keep.shape[0]
    sums = (keep[...] + got[:count, :].astype(f32)).astype(bf16)
    mixed[:, :WIDTH] = mxu(apart(count, own), sums, 0, 0).astype(bf16)
    tail = got[count:, :STATS].astype(f32)
    block = stats[...] + (tail[:8] + tail[8:])
    high = block.astype(bf16).astype(f32)
    low = (iota((8, STATS), 0) == 7) & (iota((8, STATS), 1) >= SPARE)
    block = jnp.where(low, block - high, high)
    mixed[:, WIDTH:] = jnp.concatenate([block] * (count // 8), axis=0).astype(bf16)


def as_column(line, length):
    return jnp.transpose(jnp.broadcast_to(line, (8, line.shape[1])))[:length, 0:1]


def step_kernel(
    own,
    mixed,
    acts,
    tok,
    cot,
    squares,
    up_rows,
    up_columns,
    down_rows,
    down_columns,
    mlp_out,
    input_grad,
    step_up,
    step_down,
):
    width, units = step_up.shape
    count = acts.shape[0]
    sums = jnp.sum(mixed[...].astype(f32).reshape(-1, 2 * own, WIDTH + STATS), axis=0)
    mlp_out[...] = sums[:own, :width].astype(bf16)
    input_grad[...] = sums[own:, :width].astype(bf16)
    block = sums[:, WIDTH:]
    rowsq_up = jnp.concatenate([block[i : i + 1] for i in range(4)], axis=1)
    colsq_down = jnp.concatenate([block[i : i + 1] for i in range(4, 8)], axis=1)
    both = block[3:4] + block[7:8]
    spare = iota((1, STATS), 1)
    total_up, total_down, total_rows = (
        jnp.sum(jnp.where(spare == SPARE + i, both, 0.0), axis=1, keepdims=True) for i in range(3)
    )
    digits = acts[0:16, SLOPE:].astype(f32)[0:1]
    lane = iota((1, UNITS), 1)
    weight = jnp.zeros((1, UNITS), f32)
    for digit in range(DIGITS):
        weight = jnp.where(lane == units + 1 + digit, 2.0 * 16.0**digit / DIGIT_UNIT, weight)
    total_state = jnp.sum(digits * weight, axis=1, keepdims=True)
    mean_up = (decay_rate * total_state + (1.0 - decay_rate) * total_up / FF) / D
    mean_down = (decay_rate * total_rows + (1.0 - decay_rate) * total_down / D) / FF
    keep_rate = 1.0 - decay_rate
    row_new_up = decay_rate * up_rows[...] + keep_rate * rowsq_up[:, :width] / FF
    col_new_down = decay_rate * down_columns[...] + keep_rate * colsq_down[:, :width] / FF
    col_new_up = decay_rate * up_columns[...] + keep_rate * squares[0:1, :units] / D
    row_new_down = decay_rate * down_rows[...] + keep_rate * squares[1:2, :units] / D
    row_up = jnp.concatenate(
        [lax.rsqrt(row_new_up / mean_up), jnp.zeros((1, WIDTH - width), f32)], axis=1
    )
    row_down = jnp.concatenate(
        [lax.rsqrt(row_new_down / mean_down), jnp.zeros((1, UNITS - units), f32)], axis=1
    )
    g_up = mxu(tok[...], acts[:, SLOPE:], 0, 0)[:width, :units]
    step_up[...] = (g_up * as_column(row_up, width) * lax.rsqrt(col_new_up)).astype(bf16)
    g_down = mxu(acts[:, :UNITS], cot[...], 0, 0)[:units, :width]
    step_down[...] = (g_down * as_column(row_down, units) * lax.rsqrt(col_new_down)).astype(bf16)


def on_device(
    tokens,
    cotangent,
    codes_up,
    scales_up,
    codes_down,
    scales_down,
    up_rows,
    up_columns,
    down_rows,
    down_columns,
):
    width, units = codes_up.shape
    own = tokens.shape[0]
    wide = lax.axis_size("wide")
    narrow = lax.axis_size("narrow")
    chips = narrow // 2
    line = wide // 2
    count = own * narrow
    core_pairs = [(i, i ^ 1) for i in range(narrow)]
    same_core = [[2 * i + core for i in range(chips)] for core in range(2)]
    half_pairs = [(i, i ^ 1) for i in range(wide)]
    same_half = [[2 * i + half for i in range(line)] for half in range(2)]
    up_rows, down_rows = up_rows[None], down_rows[None]
    up_columns, down_columns = up_columns[None], down_columns[None]

    packed = jnp.concatenate([tokens, cotangent], axis=0)
    mine = lax.all_to_all(
        jnp.broadcast_to(packed[None], (chips,) + packed.shape),
        "narrow",
        0,
        0,
        axis_index_groups=same_core,
    ).reshape(count, width)
    w_up, w_down = whole_call(
        weights_kernel, [((WIDTH, UNITS), bf16), ((UNITS, WIDTH), bf16)], "weights"
    )(codes_up, scales_up, codes_down, scales_down)
    mine, w_up, w_down = lax.optimization_barrier((mine, w_up, w_down))
    other = lax.ppermute(mine, "narrow", core_pairs)
    tok, cot, parts = whole_call(
        functools.partial(partial_kernel, own),
        [((count, WIDTH), bf16), ((count, WIDTH), bf16), ((count, LANES), bf16)],
        "partial_sums",
    )(mine, other, w_up, w_down, up_rows)

    parts = lax.all_to_all(
        parts.reshape(line, -1, LANES), "wide", 0, 0, axis_index_groups=same_half
    )
    sums = jnp.sum(parts.astype(f32), axis=0)
    sums = sums + lax.ppermute(sums.astype(bf16), "wide", half_pairs).astype(f32)
    pre = sums[:, :UNITS]
    acts = jnp.concatenate(
        [gelu_value(pre), sums[:, UNITS:SLOPE], sums[:, SLOPE:] * gelu_slope(pre)], axis=1
    ).astype(bf16)
    acts = lax.all_to_all(
        jnp.broadcast_to(acts[None], (line,) + acts.shape),
        "wide",
        0,
        0,
        axis_index_groups=same_half,
    ).reshape(count, LANES)

    send, keep, stats, squares = whole_call(
        functools.partial(mix_kernel, units),
        [
            ((count + 16, WIDTH), bf16),
            ((count, WIDTH), f32),
            ((8, STATS), f32),
            ((2, UNITS), f32),
        ],
        "outputs_and_squares",
    )(acts, tok, cot, w_up, w_down, down_rows)
    got = lax.ppermute(send, "narrow", core_pairs)
    (mixed,) = whole_call(
        functools.partial(pair_kernel, own), [((count, WIDTH + STATS), bf16)], "pair_sum"
    )(keep, got, stats)
    mixed = lax.all_to_all(
        mixed.reshape(chips, -1, WIDTH + STATS), "narrow", 0, 0, axis_index_groups=same_core
    ).reshape(count, WIDTH + STATS)
    return tuple(
        whole_call(
            functools.partial(step_kernel, own),
            [
                ((own, width), bf16),
                ((own, width), bf16),
                ((width, units), bf16),
                ((units, width), bf16),
            ],
            "steps",
        )(mixed, acts, tok, cot, squares, up_rows, up_columns, down_rows, down_columns)
    )


def solution(mesh):
    return jax.shard_map(
        on_device,
        mesh=mesh,
        in_specs=(
            P("narrow", "wide"),
            P("narrow", "wide"),
            P("wide", "narrow"),
            P("wide", "narrow"),
            P("narrow", "wide"),
            P("narrow", "wide"),
            P("wide"),
            P("narrow"),
            P("narrow"),
            P("wide"),
        ),
        out_specs=(
            P("narrow", "wide"),
            P("narrow", "wide"),
            P("wide", "narrow"),
            P("narrow", "wide"),
        ),
        check_vma=False,
    )
```

time: 754 us -> 143 us (0.19)
  the two profiles are of different devices: /device:TPU:16 before, /device:TPU:2 now
where the time goes in v2:
time: 143 us; the launch traced here: 142 us
  blocking collectives  76.2 us (53%)
  starting transfers between devices  33.1 us (23%)
  waiting for transfers between devices  18.4 us (13%)
  Pallas kernels  7.21 us (5%)
  local copies, waits for them, and re-layouts  5.79 us (4%)
    all_to_all x1, blocking collectives, on_device(): lax.all_to_all(parts.reshape(line, -1, LANES), 'wide', 0, 0, axis_index_g...  27.9 us
    all_to_all x1, blocking collectives, on_device(): lax.all_to_all(mixed.reshape(chips, -1, WIDTH + STATS), 'narrow', 0, 0, a...  27.3 us
    all_to_all x1, blocking collectives, on_device(): lax.all_to_all(jnp.broadcast_to(acts[None], (line,) + acts.shape), 'wide'...  21 us
    all_to_all x1, starting transfers between devices, on_device(): lax.all_to_all(jnp.broadcast_to(packed[None], (chips,) + packed.shape), '...  17.4 us
    all_to_all x1, waiting for transfers between devices, on_device(): lax.all_to_all(jnp.broadcast_to(packed[None], (chips,) + packed.shape), '...  12 us
    ppermute x1, starting transfers between devices, on_device(): lax.ppermute(sums.astype(bf16), 'wide', half_pairs).astype(f32)  11.9 us
    pallas_call x5, Pallas kernels, whole_call(): pl.pallas_call(kernel, out_shape=[jax.ShapeDtypeStruct(shape, dtype) for...  7.21 us
    unnamed x20, local copies, waits for them, and re-layouts  3.55 us
  transfers between devices with their start and end apart: 4, of which 4 were waited for; matrix products, arithmetic and copies ran while one was open for 1% of the time, Pallas kernels for 1%

profile of v2, /device:TPU:2, one launch (start us, length us, event | category | flops | bytes accessed | tf_op | source)
XLA Modules:
  0.0 142.4 jit_solution(15670948982977325938)
XLA Ops:
  0.6 0.7 pad_maximum_fusion.1
  1.4 0.0 copy-start.7
  1.4 0.9 broadcast_in_dim.24
  2.2 17.4 %all-to-all-start = ((bf16[32,8,928]{2,1,0:T(8,128)(2,1)}), bf16[32,8,928]{2,1,0:T(8,128)(2,1)}, u32[]{:S(2)}, u32[]{:S(2)}) async-start(bf16[32,8,928]{2,1,0:T(8,128)(2,1)} %broadcast_in_dim.24), calls=%async_computation | async-start | bytes 1048576 | tf_op jit(solution)/shard_map/all_to_all | solution.py:268
  19.6 0.2 copy.14.scales_up
  19.9 0.7 copy.15.codes_down
  20.5 0.0 copy-start
  20.6 1.2 copy-done
  21.7 0.8 copy-done.1
  22.5 1.0 weights.1
  23.5 12.0 %all-to-all-done = bf16[32,8,928]{2,1,0:T(8,128)(2,1)} async-done(((bf16[32,8,928]{2,1,0:T(8,128)(2,1)}), bf16[32,8,928]{2,1,0:T(8,128)(2,1)}, u32[]{:S(2)}, u32[]{:S(2)}) %all-to-all-start) | async-done | bytes 475168 | tf_op jit(solution)/shard_map/all_to_all | solution.py:268
  35.5 1.9 %collective-permute-start = (bf16[256,928]{1,0:T(8,128)(2,1)}, bf16[256,928]{1,0:T(8,128)(2,1)S(1)}, u32[]{:S(2)}, u32[]{:S(2)}) collective-permute-start(bf16[256,928]{1,0:T(8,128)(2,1)} %bitcast.mine), channel_id=1, source_target_pairs={{0,1},{1,0},{2,3},{3,2},{4,5},{5,4},{6,7},{7,6},{8,9},{9,8},{10,11... | collective-permute-start | bytes 1425416 | tf_op jit(solution)/shard_map/ppermute | solution.py:279
  37.4 2.1 %collective-permute-done.other = bf16[256,928]{1,0:T(8,128)(2,1)S(1)} collective-permute-done((bf16[256,928]{1,0:T(8,128)(2,1)}, bf16[256,928]{1,0:T(8,128)(2,1)S(1)}, u32[]{:S(2)}, u32[]{:S(2)}) %collective-permute-start) | collective-permute-done | bytes 475168 | tf_op jit(solution)/shard_map/ppermute | solution.py:279
  39.5 0.7 copy-done.2
  40.2 2.3 %partial_sums.1 = (bf16[256,1024]{1,0:T(8,128)(2,1)S(1)}, bf16[256,1024]{1,0:T(8,128)(2,1)S(1)}, bf16[256,1280]{1,0:T(8,128)(2,1)S(1)}) custom-call(bf16[256,928]{1,0:T(8,128)(2,1)} %bitcast.mine, bf16[256,928]{1,0:T(8,128)(2,1)S(1)} %collective-permute-done.other, bf16[1024,512]{1,0:T(8,128)(2,1)S(1)} %get-tuple-element.19.w_up, ...), custom_call_target="tpu_custom_call" | custom-call | tf_op jit(solution)/shard_map/partial_sums/pallas_call | solution.py:54
  42.5 27.9 %all_to_all.20 = bf16[8,32,1280]{2,1,0:T(8,128)(2,1)S(1)} all-to-all(bf16[8,32,1280]{2,1,0:T(8,128)(2,1)S(1)} %bitcast.13), channel_id=1, replica_groups={{0,128,256,384,512,640,768,896},{64,192,320,448,576,704,832,960},{1,129..., dimensions={0} | all-to-all | bytes 1310720 | tf_op jit(solution)/shard_map/all_to_all | solution.py:286
  70.4 0.1 convert_reduce_fusion
  70.5 11.9 %collective-permute-start.1 = (bf16[32,1280]{1,0:T(8,128)(2,1)S(1)}, bf16[32,1280]{1,0:T(8,128)(2,1)S(1)}, u32[]{:S(2)}, u32[]{:S(2)}) collective-permute-start(bf16[32,1280]{1,0:T(8,128)(2,1)S(1)} %convert_element_type.15), channel_id=1, source_target_pairs={{0,64},{64,0},{128,192},{192,128},{256,320},{320,256},{384,448},{4... | collective-permute-start | bytes 245768 | tf_op jit(solution)/shard_map/ppermute | solution.py:290
  82.4 2.4 %collective-permute-done.1 = bf16[32,1280]{1,0:T(8,128)(2,1)S(1)} collective-permute-done((bf16[32,1280]{1,0:T(8,128)(2,1)S(1)}, bf16[32,1280]{1,0:T(8,128)(2,1)S(1)}, u32[]{:S(2)}, u32[]{:S(2)}) %collective-permute-start.1) | collective-permute-done | bytes 81952 | tf_op jit(solution)/shard_map/ppermute | solution.py:290
  84.9 0.0 copy-start.4
  84.9 21.0 %all_to_all.21 = bf16[8,32,1280]{2,1,0:T(8,128)(2,1)S(1)} all-to-all(bf16[8,32,1280]{2,1,0:T(8,128)(2,1)S(1)} %broadcast_in_dim.26), channel_id=1, replica_groups={{0,128,256,384,512,640,768,896},{64,192,320,448,576,704,832,960},{1,129..., dimensions={0} | all-to-all | bytes 1310720 | tf_op jit(solution)/shard_map/all_to_all | solution.py:295
  106.0 1.5 %outputs_and_squares.1 = (bf16[272,1024]{1,0:T(8,128)(2,1)S(1)}, f32[256,1024]{1,0:T(8,128)S(1)}, f32[8,256]{1,0:T(8,128)S(1)}, f32[2,512]{1,0:T(2,128)S(1)}) custom-call(bf16[256,1280]{1,0:T(8,128)(2,1)S(1)} %bitcast.9, bf16[256,1024]{1,0:T(8,128)(2,1)S(1)} %get-tuple-element.22.tok, bf16[256,1024]{1,0:T(8,128)(2,1)S(1)} %get-tuple-element.23.cot, ...), custom_call_target="tpu_custom_call" | custom-call | tf_op jit(solution)/shard_map/outputs_and_squares/pallas_call | solution.py:54
  107.4 1.9 %collective-permute-start.2 = (bf16[272,1024]{1,0:T(8,128)(2,1)S(1)}, bf16[272,1024]{1,0:T(8,128)(2,1)S(1)}, u32[]{:S(2)}, u32[]{:S(2)}) collective-permute-start(bf16[272,1024]{1,0:T(8,128)(2,1)S(1)} %get-tuple-element.25), channel_id=1, source_target_pairs={{0,1},{1,0},{2,3},{3,2},{4,5},{5,4},{6,7},{7,6},{8,9},{9,8},{10,11... | collective-permute-start | bytes 1671176 | tf_op jit(solution)/shard_map/ppermute | solution.py:313
  109.4 1.9 %collective-permute-done.2.got = bf16[272,1024]{1,0:T(8,128)(2,1)S(1)} collective-permute-done((bf16[272,1024]{1,0:T(8,128)(2,1)S(1)}, bf16[272,1024]{1,0:T(8,128)(2,1)S(1)}, u32[]{:S(2)}, u32[]{:S(2)}) %collective-permute-start.2) | collective-permute-done | bytes 557088 | tf_op jit(solution)/shard_map/ppermute | solution.py:313
  111.3 0.4 pair_sum.1
  111.7 0.0 copy-start.3
  111.7 0.0 copy-start.5
  111.7 0.0 copy-start.6
  111.7 27.3 %all_to_all.22 = bf16[32,8,1280]{2,1,0:T(8,128)(2,1)S(1)} all-to-all(bf16[32,8,1280]{2,1,0:T(8,128)(2,1)S(1)} %bitcast.12), channel_id=1, replica_groups={{0,2,4,6,8,10,12,14,16,18,20,22,24,26,28,30,32,34,36,38,40,42,44,46,48,..., dimensions={0} | all-to-all | bytes 1310720 | tf_op jit(solution)/shard_map/all_to_all | solution.py:317
  139.0 0.0 copy-done.3
  139.0 2.1 %steps.1 = (bf16[4,928]{1,0:T(4,128)(2,1)}, bf16[4,928]{1,0:T(4,128)(2,1)}, bf16[928,480]{1,0:T(8,128)(2,1)}, bf16[480,928]{1,0:T(8,128)(2,1)S(1)}) custom-call(bf16[256,1280]{1,0:T(8,128)(2,1)S(1)} %bitcast.11, bf16[256,1280]{1,0:T(8,128)(2,1)S(1)} %bitcast.10, bf16[256,1024]{1,0:T(8,128)(2,1)S(1)} %get-tuple-element.22.tok, ...), custom_call_target="tpu_custom_call" | custom-call | tf_op jit(solution)/shard_map/steps/pallas_call | solution.py:54
  141.1 1.3 copy.16
  (14 shorter events, 0.1 us)
Async XLA Ops:
  0.6 19.0 %copy-start.8 = (f32[928,5]{0,1:T(8,128)S(1)}, f32[928,5]{0,1:T(8,128)}, u32[]{:S(2)}) copy-start(f32[928,5]{0,1:T(8,128)} %param.13) | copy-start | bytes 55684
  1.4 18.5 %copy-start.7 = (bf16[480,928]{0,1:T(8,128)(2,1)S(1)}, bf16[480,928]{0,1:T(8,128)(2,1)}, u32[]{:S(2)}) copy-start(bf16[480,928]{0,1:T(8,128)(2,1)} %param.14) | copy-start | bytes 2672644
  2.2 33.3 %all-to-all-start = ((bf16[32,8,928]{2,1,0:T(8,128)(2,1)}), bf16[32,8,928]{2,1,0:T(8,128)(2,1)}, u32[]{:S(2)}, u32[]{:S(2)}) async-start(bf16[32,8,928]{2,1,0:T(8,128)(2,1)} %broadcast_in_dim.24), calls=%async_computation | async-start | bytes 1048576 | tf_op jit(solution)/shard_map/all_to_all | solution.py:268
  20.5 1.2 copy-start
  21.7 0.8 copy-start.1
  35.5 4.0 %collective-permute-start = (bf16[256,928]{1,0:T(8,128)(2,1)}, bf16[256,928]{1,0:T(8,128)(2,1)S(1)}, u32[]{:S(2)}, u32[]{:S(2)}) collective-permute-start(bf16[256,928]{1,0:T(8,128)(2,1)} %bitcast.mine), channel_id=1, source_target_pairs={{0,1},{1,0},{2,3},{3,2},{4,5},{5,4},{6,7},{7,6},{8,9},{9,8},{10,11... | collective-permute-start | bytes 1425416 | tf_op jit(solution)/shard_map/ppermute | solution.py:279
  39.5 0.7 copy-start.2
  70.5 14.3 %collective-permute-start.1 = (bf16[32,1280]{1,0:T(8,128)(2,1)S(1)}, bf16[32,1280]{1,0:T(8,128)(2,1)S(1)}, u32[]{:S(2)}, u32[]{:S(2)}) collective-permute-start(bf16[32,1280]{1,0:T(8,128)(2,1)S(1)} %convert_element_type.15), channel_id=1, source_target_pairs={{0,64},{64,0},{128,192},{192,128},{256,320},{320,256},{384,448},{4... | collective-permute-start | bytes 245768 | tf_op jit(solution)/shard_map/ppermute | solution.py:290
  84.9 21.1 %copy-start.4 = (f32[480]{0:T(512)S(1)}, f32[480]{0:T(512)}, u32[]{:S(2)}) copy-start(f32[480]{0:T(512)} %param.18) | copy-start | bytes 5764
  107.4 3.9 %collective-permute-start.2 = (bf16[272,1024]{1,0:T(8,128)(2,1)S(1)}, bf16[272,1024]{1,0:T(8,128)(2,1)S(1)}, u32[]{:S(2)}, u32[]{:S(2)}) collective-permute-start(bf16[272,1024]{1,0:T(8,128)(2,1)S(1)} %get-tuple-element.25), channel_id=1, source_target_pairs={{0,1},{1,0},{2,3},{3,2},{4,5},{5,4},{6,7},{7,6},{8,9},{9,8},{10,11... | collective-permute-start | bytes 1671176 | tf_op jit(solution)/shard_map/ppermute | solution.py:313
  111.7 27.3 %copy-start.3 = (f32[928]{0:T(1024)S(1)}, f32[928]{0:T(1024)}, u32[]{:S(2)}) copy-start(f32[928]{0:T(1024)} %param.16) | copy-start | bytes 11140
  111.7 27.3 %copy-start.5 = (f32[928]{0:T(1024)S(1)}, f32[928]{0:T(1024)}, u32[]{:S(2)}) copy-start(f32[928]{0:T(1024)} %param.19) | copy-start | bytes 11140
  111.7 27.3 %copy-start.6 = (f32[480]{0:T(512)S(1)}, f32[480]{0:T(512)}, u32[]{:S(2)}) copy-start(f32[480]{0:T(512)} %param.17) | copy-start | bytes 5764

commit v3 on v2

v3 whole, which is shorter than its diff:
```python
import functools

import jax
import jax.numpy as jnp
from jax import lax
from jax.experimental import pallas as pl
from jax.experimental.pallas import tpu as pltpu
from jax.sharding import PartitionSpec as P

D = 14848
FF = 30720
QB = 96

decay_rate = 0.9
square_eps = 1e-30

bf16 = jnp.bfloat16
f32 = jnp.float32

WIDTH = 1024
UNITS = 512
GRAM = 256
SLOPE = UNITS + GRAM
LANES = SLOPE + UNITS
DIGITS = 6
DIGIT_UNIT = 8.0
STATS = 256
SPARE = 160
CHUNK = 256


def gelu_value(value):
    return 0.5 * value * (1.0 + lax.erf(value * 0.7071067811865476))


def gelu_slope(value):
    return (
        0.5 * (1.0 + lax.erf(value * 0.7071067811865476))
        + value * jnp.exp(-0.5 * value * value) * 0.3989422804014327
    )


def mxu(left, right, left_dim=1, right_dim=0):
    return lax.dot_general(
        left, right, (((left_dim,), (right_dim,)), ((), ())), preferred_element_type=f32
    )


def iota(shape, dim):
    return lax.broadcasted_iota(jnp.int32, shape, dim)


def whole_call(kernel, outs, name, flops=0, scratch=(), out_spaces=None):
    spec = pl.BlockSpec(memory_space=pltpu.VMEM)
    spaces = out_spaces or [pltpu.VMEM] * len(outs)

    def call(*args):
        moved = sum(a.size * a.dtype.itemsize for a in args)
        return pl.pallas_call(
            kernel,
            out_shape=[jax.ShapeDtypeStruct(shape, dtype) for shape, dtype in outs],
            in_specs=[spec] * len(args),
            out_specs=[pl.BlockSpec(memory_space=space) for space in spaces],
            scratch_shapes=list(scratch),
            compiler_params=pltpu.CompilerParams(vmem_limit_bytes=24 * 1024 * 1024),
            cost_estimate=pl.CostEstimate(flops=flops, bytes_accessed=moved, transcendentals=0),
            name=name,
        )(*args)

    return call


def spread_kernel(packed, copies):
    both = packed[...].astype(f32)
    both = jnp.concatenate([both, both], axis=0).astype(bf16)
    for pair in range(copies.shape[0] // 16):
        copies[16 * pair : 16 * pair + 16, :] = both


def weights_kernel(codes_up, scales_up, codes_down, scales_down, up_rows, w_up, w_down, digits, lines):
    width, units = codes_up.shape
    lane = iota((width, units), 1)
    for codes, scales, ref in ((codes_up, scales_up, w_up), (codes_down, scales_down, w_down)):
        lines[...] = jnp.zeros_like(lines)
        lines[: units // QB, :width] = scales[...]
        columns = jnp.transpose(lines[...])[:width]
        spread = columns[:, 0:1]
        for group in range(1, units // QB):
            spread = jnp.where(lane >= group * QB, columns[:, group : group + 1], spread)
        ref[...] = jnp.zeros_like(ref)
        ref[:width, :units] = (codes[...].astype(f32) * spread).astype(bf16)
    place = iota((8, UNITS), 1)
    line = jnp.zeros((8, UNITS), f32)
    rest = jnp.floor(jnp.sum(up_rows[...], axis=1, keepdims=True) * DIGIT_UNIT + 0.5)
    for digit in range(DIGITS):
        shorter = jnp.floor(rest * (1.0 / 16.0))
        line = jnp.where(place == units + 1 + digit, rest - 16.0 * shorter, line)
        rest = shorter
    digits[...] = line


def apart(count, own):
    half = count // 2
    row, column = iota((count, count), 0), iota((count, count), 1)
    second = (row >= half).astype(jnp.int32)
    token = row - second * half
    source = (token // own) * (2 * own) + second * own + token % own
    return (column == source).astype(f32).astype(bf16)


def first_kernel(own, mine, w_up, w_down, tok, cot, pre, slope):
    count, width = mine.shape
    half = count // 2
    rows = mxu(apart(count, own), mine[...]).astype(bf16)
    for ref, first in ((tok, 0), (cot, half)):
        ref[:, WIDTH - 128 :] = jnp.zeros((half, 128), bf16)
        ref[:, :width] = rows[first : first + half]
    pre[...] = mxu(tok[...], w_up[...]).astype(bf16)
    slope[...] = mxu(cot[...], w_down[...])


def partial_kernel(
    own, units, other, tok_own, cot_own, pre_own, slope_own, w_up, w_down, digits, tok, cot, parts
):
    count, width = other.shape
    half = count // 2
    rows = mxu(apart(count, own), other[...]).astype(bf16)
    for ref, first, owned in ((tok, 0, tok_own), (cot, half, cot_own)):
        ref[:half, :] = owned[...]
        ref[half:, WIDTH - 128 :] = jnp.zeros((half, 128), bf16)
        ref[half:, :width] = rows[first : first + half]
    parts[:half, :UNITS] = pre_own[...]
    parts[half:, :UNITS] = mxu(tok[half:, :], w_up[...]).astype(bf16)
    row, column = iota((count, count), 0), iota((count, count), 1)
    tokens, cotangents = tok[...], cot[...]
    gram_tok = mxu(tokens, tokens, 1, 1)
    gram_cot = mxu(cotangents, cotangents, 1, 1)
    parts[:, UNITS:SLOPE] = jnp.where(row >= column, gram_tok, gram_cot).astype(bf16)
    diagonal = jnp.sum(jnp.where(row == column, gram_cot, 0.0), axis=1, keepdims=True)
    lane = iota((half, UNITS), 1)
    extra = digits[0:1, :]
    slope = jnp.where(lane == units, diagonal[:half], slope_own[...] + extra)
    parts[:half, SLOPE:] = slope.astype(bf16)
    slope = mxu(cot[half:, :], w_down[...])
    slope = jnp.where(lane == units, diagonal[half:], slope + extra)
    parts[half:, SLOPE:] = slope.astype(bf16)


def masked_slope(acts, units):
    count = acts.shape[0]
    lane = iota((count, UNITS), 1)
    return jnp.where(lane < units, acts[:, SLOPE:].astype(f32), 0.0)


def send_kernel(units, acts, tok, cot, w_up, w_down, down_rows, send, stats, squares):
    count = acts.shape[0]
    half = count // 2
    hidden = acts[:, :UNITS]
    d_wide = masked_slope(acts, units)
    diagonal = 2.0 * acts[:, SLOPE:].astype(f32)[:, units : units + 1]
    d_pre = d_wide.astype(bf16)
    send[:half, :] = mxu(hidden[half:], w_down[...], 1, 1).astype(bf16)
    send[half:count, :] = mxu(d_pre[half:], w_up[...], 1, 1).astype(bf16)
    row, column = iota((count, count), 0), iota((count, count), 1)
    gram = acts[:, UNITS:SLOPE].astype(f32)
    lower = jnp.where(row > column, 2.0 * gram, jnp.where(row == column, gram, 0.0)).astype(bf16)
    upper = jnp.where(row < column, 2.0 * gram, 0.0).astype(bf16)
    hidden_wide = hidden.astype(f32)
    colsq_up = jnp.sum(d_wide * mxu(lower, d_pre), axis=0, keepdims=True)
    rowsq_down = jnp.sum(
        hidden_wide * (mxu(upper, hidden) + diagonal * hidden_wide), axis=0, keepdims=True
    )
    real = iota((1, UNITS), 1) < units
    colsq_up = jnp.where(real, jnp.maximum(colsq_up, 0.0) + D * square_eps, 0.0)
    rowsq_down = jnp.where(real, jnp.maximum(rowsq_down, 0.0) + D * square_eps, 0.0)
    squares[0:1, :] = colsq_up
    squares[1:2, :] = rowsq_down
    totals = [
        jnp.sum(colsq_up, axis=1, keepdims=True),
        jnp.sum(rowsq_down, axis=1, keepdims=True),
        jnp.sum(down_rows[...], axis=1, keepdims=True),
    ]
    g_up = mxu(d_pre, tok[...], 0, 0)
    rowsq_up = jnp.sum(g_up * g_up, axis=0, keepdims=True) + units * square_eps
    g_down = mxu(hidden, cot[...], 0, 0)
    colsq_down = jnp.sum(g_down * g_down, axis=0, keepdims=True) + units * square_eps
    spare = iota((1, STATS), 1)
    for place, sums in ((0, rowsq_up), (4, colsq_down)):
        for part in range(4):
            piece = sums[:, part * STATS : (part + 1) * STATS]
            if part == 3:
                piece = jnp.where(spare < SPARE, piece, 0.0)
                for index, total in enumerate(totals):
                    piece = jnp.where(spare == SPARE + index, total, piece)
            stats[place + part : place + part + 1, :] = piece
    block = stats[...]
    high = block.astype(bf16).astype(f32)
    send[count:, :] = jnp.zeros((16, WIDTH), bf16)
    send[count:, :STATS] = jnp.concatenate([high, block - high], axis=0).astype(bf16)


def keep_kernel(units, acts, w_up, w_down, keep):
    half = acts.shape[0] // 2
    keep[:half, :] = mxu(acts[:half, :UNITS], w_down[...], 1, 1)
    d_pre = masked_slope(acts, units)[:half].astype(bf16)
    keep[half:, :] = mxu(d_pre, w_up[...], 1, 1)


def pair_kernel(own, keep, got, stats, mixed):
    count = keep.shape[0]
    sums = (keep[...] + got[:count, :].astype(f32)).astype(bf16)
    mixed[:, :WIDTH] = mxu(apart(count, own), sums, 0, 0).astype(bf16)
    tail = got[count:, :STATS].astype(f32)
    block = stats[...] + (tail[:8] + tail[8:])
    high = block.astype(bf16).astype(f32)
    low = (iota((8, STATS), 0) == 7) & (iota((8, STATS), 1) >= SPARE)
    block = jnp.where(low, block - high, high)
    mixed[:, WIDTH:] = jnp.concatenate([block] * (count // 8), axis=0).astype(bf16)


def padded(line, lanes):
    return jnp.concatenate([line, jnp.ones((1, lanes - line.shape[1]), f32)], axis=1)


def step_kernel(
    own,
    units,
    mixed,
    acts,
    tok,
    cot,
    squares,
    up_rows,
    up_columns,
    down_rows,
    down_columns,
    mlp_out,
    input_grad,
    step_up,
    step_down,
    held,
    sems,
):
    width = up_rows.shape[1]
    sums = jnp.sum(mixed[...].astype(f32).reshape(-1, 2 * own, WIDTH + STATS), axis=0)
    mlp_out[...] = sums[:own, :width].astype(bf16)
    input_grad[...] = sums[own:, :width].astype(bf16)
    block = sums[:, WIDTH:]
    rowsq_up = jnp.concatenate([block[i : i + 1] for i in range(4)], axis=1)
    colsq_down = jnp.concatenate([block[i : i + 1] for i in range(4, 8)], axis=1)
    both = block[3:4] + block[7:8]
    spare = iota((1, STATS), 1)
    total_up, total_down, total_rows = (
        jnp.sum(jnp.where(spare == SPARE + i, both, 0.0), axis=1, keepdims=True) for i in range(3)
    )
    digits = acts[0:16, SLOPE:].astype(f32)[0:1]
    lane = iota((1, UNITS), 1)
    weight = jnp.zeros((1, UNITS), f32)
    for digit in range(DIGITS):
        weight = jnp.where(lane == units + 1 + digit, 2.0 * 16.0**digit / DIGIT_UNIT, weight)
    total_state = jnp.sum(digits * weight, axis=1, keepdims=True)
    mean_up = (decay_rate * total_state + (1.0 - decay_rate) * total_up / FF) / D
    mean_down = (decay_rate * total_rows + (1.0 - decay_rate) * total_down / D) / FF
    keep_rate = 1.0 - decay_rate
    row_new_up = decay_rate * up_rows[...] + keep_rate * rowsq_up[:, :width] / FF
    col_new_down = decay_rate * down_columns[...] + keep_rate * colsq_down[:, :width] / FF
    lines = jnp.concatenate(
        [
            jnp.broadcast_to(padded(lax.rsqrt(row_new_up) * jnp.sqrt(mean_up), WIDTH), (4, WIDTH)),
            jnp.broadcast_to(
                padded(lax.rsqrt(col_new_down) * jnp.sqrt(mean_down), WIDTH), (4, WIDTH)
            ),
        ],
        axis=0,
    )
    columns = jnp.transpose(lines)
    col_new_up = decay_rate * up_columns[...] + keep_rate * squares[0:1, :units] / D
    row_new_down = decay_rate * down_rows[...] + keep_rate * squares[1:2, :units] / D
    ups = (tok, acts[:, SLOPE:], lax.rsqrt(col_new_up), step_up)
    downs = (cot, acts[:, :UNITS], lax.rsqrt(row_new_down), step_down)
    copies = []
    for first in range(0, width, CHUNK):
        rows = slice(first, min(first + CHUNK, width))
        for which, (left, right, scale, out) in enumerate((ups, downs)):
            grads = mxu(left[:, first : first + CHUNK], right, 0, 0)
            grads = grads[: rows.stop - first, :units]
            factor = columns[rows, 4 * which : 4 * which + 1]
            held[which, rows, :] = (grads * factor * scale).astype(bf16)
            copy = pltpu.make_async_copy(
                held.at[which, rows], out.at[rows], sems.at[len(copies)]
            )
            copy.start()
            copies.append(copy)
    for copy in copies:
        copy.wait()


def on_device(
    tokens,
    cotangent,
    codes_up,
    scales_up,
    codes_down,
    scales_down,
    up_rows,
    up_columns,
    down_rows,
    down_columns,
):
    width, units = codes_up.shape
    own = tokens.shape[0]
    wide = lax.axis_size("wide")
    narrow = lax.axis_size("narrow")
    chips = narrow // 2
    line = wide // 2
    count = own * narrow
    half = count // 2
    product = 2 * half * WIDTH * UNITS
    core_pairs = [(i, i ^ 1) for i in range(narrow)]
    same_core = [[2 * i + core for i in range(chips)] for core in range(2)]
    half_pairs = [(i, i ^ 1) for i in range(wide)]
    same_half = [[2 * i + part for i in range(line)] for part in range(2)]
    up_rows, down_rows = up_rows[None], down_rows[None]
    up_columns, down_columns = up_columns[None], down_columns[None]

    (copies,) = whole_call(spread_kernel, [((count, width), bf16)], "spread")(
        jnp.concatenate([tokens, cotangent], axis=0)
    )
    mine = lax.all_to_all(
        copies.reshape(chips, 2 * own, width),
        "narrow",
        0,
        0,
        axis_index_groups=same_core,
    ).reshape(count, width)
    w_up, w_down, digits = whole_call(
        weights_kernel,
        [((WIDTH, UNITS), bf16), ((WIDTH, UNITS), bf16), ((8, UNITS), f32)],
        "weights",
        scratch=[pltpu.VMEM((8, WIDTH), f32)],
    )(codes_up, scales_up.T, codes_down.T, scales_down, up_rows)
    mine, w_up, w_down, digits = lax.optimization_barrier((mine, w_up, w_down, digits))
    other = lax.ppermute(mine, "narrow", core_pairs)
    tok_own, cot_own, pre_own, slope_own = whole_call(
        functools.partial(first_kernel, own),
        [
            ((half, WIDTH), bf16),
            ((half, WIDTH), bf16),
            ((half, UNITS), bf16),
            ((half, UNITS), f32),
        ],
        "own_partial_sums",
        flops=3 * product,
    )(mine, w_up, w_down)
    tok, cot, parts = whole_call(
        functools.partial(partial_kernel, own, units),
        [((count, WIDTH), bf16), ((count, WIDTH), bf16), ((count, LANES), bf16)],
        "partial_sums",
        flops=5 * product,
    )(other, tok_own, cot_own, pre_own, slope_own, w_up, w_down, digits)

    parts = lax.all_to_all(
        parts.reshape(line, -1, LANES), "wide", 0, 0, axis_index_groups=same_half
    )
    sums = jnp.sum(parts.astype(f32), axis=0)
    sums = sums + lax.ppermute(sums.astype(bf16), "wide", half_pairs).astype(f32)
    pre = sums[:, :UNITS]
    acts = jnp.concatenate(
        [gelu_value(pre), sums[:, UNITS:SLOPE], sums[:, SLOPE:] * gelu_slope(pre)], axis=1
    ).astype(bf16)
    acts = lax.all_to_all(
        jnp.broadcast_to(acts[None], (line,) + acts.shape),
        "wide",
        0,
        0,
        axis_index_groups=same_half,
    ).reshape(count, LANES)

    send, stats, squares = whole_call(
        functools.partial(send_kernel, units),
        [((count + 16, WIDTH), bf16), ((8, STATS), f32), ((2, UNITS), f32)],
        "outputs_and_squares",
        flops=7 * product,
    )(acts, tok, cot, w_up, w_down, down_rows)
    got = lax.ppermute(send, "narrow", core_pairs)
    (keep,) = whole_call(
        functools.partial(keep_kernel, units),
        [((count, WIDTH), f32)],
        "own_outputs",
        flops=2 * product,
    )(acts, w_up, w_down)
    (mixed,) = whole_call(
        functools.partial(pair_kernel, own), [((count, WIDTH + STATS), bf16)], "pair_sum"
    )(keep, got, stats)
    mixed = lax.all_to_all(
        mixed.reshape(chips, -1, WIDTH + STATS), "narrow", 0, 0, axis_index_groups=same_core
    ).reshape(count, WIDTH + STATS)
    mlp_out, input_grad, step_up, step_down = whole_call(
        functools.partial(step_kernel, own, units),
        [
            ((own, width), bf16),
            ((own, width), bf16),
            ((width, units), bf16),
            ((width, units), bf16),
        ],
        "steps",
        scratch=[
            pltpu.VMEM((2, width, units), bf16),
            pltpu.SemaphoreType.DMA((2 * pl.cdiv(width, CHUNK),)),
        ],
        out_spaces=[pltpu.VMEM, pltpu.VMEM, pl.ANY, pl.ANY],
    )(mixed, acts, tok, cot, squares, up_rows, up_columns, down_rows, down_columns)
    return mlp_out, input_grad, step_up, step_down.T


def solution(mesh):
    return jax.shard_map(
        on_device,
        mesh=mesh,
        in_specs=(
            P("narrow", "wide"),
            P("narrow", "wide"),
            P("wide", "narrow"),
            P("wide", "narrow"),
            P("narrow", "wide"),
            P("narrow", "wide"),
            P("wide"),
            P("narrow"),
            P("narrow"),
            P("wide"),
        ),
        out_specs=(
            P("narrow", "wide"),
            P("narrow", "wide"),
            P("wide", "narrow"),
            P("narrow", "wide"),
        ),
        check_vma=False,
    )
```

time: 143 us -> 140 us (0.979)
  local copies, waits for them, and re-layouts: 5.79 us -> 2.46 us
  Pallas kernels: 7.21 us -> 9.6 us
    pallas_call x5 -> x8, Pallas kernels: 7.21 us -> 9.6 us  [call(): pl.pallas_call(kernel, out_shape=[jax.ShapeDtypeStruct(shape, dtype) for...]
    unnamed x20 -> x16, local copies, waits for them, and re-layouts: 3.55 us -> 2.41 us
  transfers between devices with their start and end apart: 4 -> 4, of which waited for: 4 -> 4; matrix products, arithmetic and copies ran while one was open for 1% -> 0% of each run, Pallas kernels for 1% -> 2%
where the time goes in v3:
time: 140 us; the launch traced here: 139 us
  blocking collectives  76.1 us (54%)
  starting transfers between devices  32.4 us (23%)
  waiting for transfers between devices  17.1 us (12%)
  Pallas kernels  9.6 us (7%)
  local copies, waits for them, and re-layouts  2.46 us (2%)
    all_to_all x1, blocking collectives, on_device(): lax.all_to_all(parts.reshape(line, -1, LANES), 'wide', 0, 0, axis_index_g...  27.9 us
    all_to_all x1, blocking collectives, on_device(): lax.all_to_all(mixed.reshape(chips, -1, WIDTH + STATS), 'narrow', 0, 0, a...  27.2 us
    all_to_all x1, blocking collectives, on_device(): lax.all_to_all(jnp.broadcast_to(acts[None], (line,) + acts.shape), 'wide'...  21 us
    all_to_all x1, starting transfers between devices, on_device(): lax.all_to_all(copies.reshape(chips, 2 * own, width), 'narrow', 0, 0, axi...  16.7 us
    all_to_all x1, waiting for transfers between devices, on_device(): lax.all_to_all(copies.reshape(chips, 2 * own, width), 'narrow', 0, 0, axi...  12.3 us
    ppermute x1, starting transfers between devices, on_device(): lax.ppermute(sums.astype(bf16), 'wide', half_pairs).astype(f32)  11.9 us
    pallas_call x8, Pallas kernels, call(): pl.pallas_call(kernel, out_shape=[jax.ShapeDtypeStruct(shape, dtype) for...  9.6 us
  transfers between devices with their start and end apart: 4, of which 4 were waited for; matrix products, arithmetic and copies ran while one was open for 0% of the time, Pallas kernels for 2%

profile of v3, /device:TPU:2, one launch (start us, length us, event | category | flops | bytes accessed | tf_op | source)
XLA Modules:
  0.0 139.4 jit_solution(16840840470749628198)
XLA Ops:
  0.6 0.0 copy-start.4
  0.7 0.7 pad_maximum_fusion.1.packed
  1.4 0.9 spread.1
  2.3 16.7 %all-to-all-start = ((bf16[32,8,928]{2,1,0:T(8,128)(2,1)}), bf16[32,8,928]{2,1,0:T(8,128)(2,1)S(1)}, u32[]{:S(2)}, u32[]{:S(2)}) async-start(bf16[32,8,928]{2,1,0:T(8,128)(2,1)} %bitcast), calls=%async_computation | async-start | bytes 1048576 | tf_op jit(solution)/shard_map/all_to_all | solution.py:329
  19.0 0.0 copy-done.4
  19.0 0.0 copy-done.3
  19.0 0.0 copy-done.2
  19.0 0.0 copy-start
  19.0 1.2 copy-done
  20.2 1.2 copy-done.1
  21.4 1.7 %weights.1 = (bf16[1024,512]{1,0:T(8,128)(2,1)S(1)}, bf16[1024,512]{1,0:T(8,128)(2,1)S(1)}, f32[8,512]{1,0:T(8,128)S(1)}) custom-call(bf16[928,480]{1,0:T(8,128)(2,1)S(1)} %copy-done, f32[5,928]{1,0:T(8,128)S(1)} %bitcast.22, bf16[928,480]{1,0:T(8,128)(2,1)S(1)} %bitcast.20, f32[5,928]{1,0:T(8,128)S(1)} %copy-done.3, f32[1,928]{1,0:T(1,128)S(1)} %bitcast.23), custom_call_target="tpu_custom_call" | custom-call | bytes 1822592 | tf_op jit(solution)/shard_map/weights/pallas_call | solution.py:59
  23.1 12.3 %all-to-all-done = bf16[32,8,928]{2,1,0:T(8,128)(2,1)S(1)} async-done(((bf16[32,8,928]{2,1,0:T(8,128)(2,1)}), bf16[32,8,928]{2,1,0:T(8,128)(2,1)S(1)}, u32[]{:S(2)}, u32[]{:S(2)}) %all-to-all-start) | async-done | bytes 475168 | tf_op jit(solution)/shard_map/all_to_all | solution.py:329
  35.4 1.9 %collective-permute-start = (bf16[256,928]{1,0:T(8,128)(2,1)S(1)}, bf16[256,928]{1,0:T(8,128)(2,1)S(1)}, u32[]{:S(2)}, u32[]{:S(2)}) collective-permute-start(bf16[256,928]{1,0:T(8,128)(2,1)S(1)} %bitcast.18), channel_id=1, source_target_pairs={{0,1},{1,0},{2,3},{3,2},{4,5},{5,4},{6,7},{7,6},{8,9},{9,8},{10,11... | collective-permute-start | bytes 1425416 | tf_op jit(solution)/shard_map/ppermute | solution.py:343
  37.3 0.6 own_partial_sums.1
  37.9 1.3 collective-permute-done.other
  39.2 0.9 partial_sums.1
  40.2 27.9 %all_to_all.20 = bf16[8,32,1280]{2,1,0:T(8,128)(2,1)S(1)} all-to-all(bf16[8,32,1280]{2,1,0:T(8,128)(2,1)S(1)} %bitcast.21), channel_id=1, replica_groups={{0,128,256,384,512,640,768,896},{64,192,320,448,576,704,832,960},{1,129..., dimensions={0} | all-to-all | bytes 1310720 | tf_op jit(solution)/shard_map/all_to_all | solution.py:362
  68.0 0.1 convert_reduce_fusion
  68.2 11.9 %collective-permute-start.1 = (bf16[32,1280]{1,0:T(8,128)(2,1)S(1)}, bf16[32,1280]{1,0:T(8,128)(2,1)S(1)}, u32[]{:S(2)}, u32[]{:S(2)}) collective-permute-start(bf16[32,1280]{1,0:T(8,128)(2,1)S(1)} %convert_element_type.15), channel_id=1, source_target_pairs={{0,64},{64,0},{128,192},{192,128},{256,320},{320,256},{384,448},{4... | collective-permute-start | bytes 245768 | tf_op jit(solution)/shard_map/ppermute | solution.py:366
  80.0 2.4 %collective-permute-done.1 = bf16[32,1280]{1,0:T(8,128)(2,1)S(1)} collective-permute-done((bf16[32,1280]{1,0:T(8,128)(2,1)S(1)}, bf16[32,1280]{1,0:T(8,128)(2,1)S(1)}, u32[]{:S(2)}, u32[]{:S(2)}) %collective-permute-start.1) | collective-permute-done | bytes 81952 | tf_op jit(solution)/shard_map/ppermute | solution.py:366
  82.5 0.0 copy-start.5
  82.6 21.0 %all_to_all.21 = bf16[8,32,1280]{2,1,0:T(8,128)(2,1)S(1)} all-to-all(bf16[8,32,1280]{2,1,0:T(8,128)(2,1)S(1)} %broadcast_in_dim.19), channel_id=1, replica_groups={{0,128,256,384,512,640,768,896},{64,192,320,448,576,704,832,960},{1,129..., dimensions={0} | all-to-all | bytes 1310720 | tf_op jit(solution)/shard_map/all_to_all | solution.py:371
  103.5 1.6 %outputs_and_squares.1 = (bf16[272,1024]{1,0:T(8,128)(2,1)S(1)}, f32[8,256]{1,0:T(8,128)S(1)}, f32[2,512]{1,0:T(2,128)S(1)}) custom-call(bf16[256,1280]{1,0:T(8,128)(2,1)S(1)} %bitcast.13, bf16[256,1024]{1,0:T(8,128)(2,1)S(1)} %get-tuple-element.37.tok, bf16[256,1024]{1,0:T(8,128)(2,1)S(1)} %get-tuple-element.38.cot, ...), custom_call_target="tpu_custom_call" | custom-call | flops 939524096 | bytes 3803008 | tf_op jit(solution)/shard_map/outputs_and_squares/pallas_call | solution.py:59
  105.1 1.9 %collective-permute-start.2 = (bf16[272,1024]{1,0:T(8,128)(2,1)S(1)}, bf16[272,1024]{1,0:T(8,128)(2,1)S(1)}, u32[]{:S(2)}, u32[]{:S(2)}) collective-permute-start(bf16[272,1024]{1,0:T(8,128)(2,1)S(1)} %get-tuple-element.39), channel_id=1, source_target_pairs={{0,1},{1,0},{2,3},{3,2},{4,5},{5,4},{6,7},{7,6},{8,9},{9,8},{10,11... | collective-permute-start | bytes 1671176 | tf_op jit(solution)/shard_map/ppermute | solution.py:385
  107.0 0.8 own_outputs.1.keep
  107.9 1.1 collective-permute-done.2.got
  109.0 0.4 pair_sum.1
  109.3 0.0 copy-start.6
  109.4 0.0 copy-start.7
  109.4 27.2 %all_to_all.22 = bf16[32,8,1280]{2,1,0:T(8,128)(2,1)S(1)} all-to-all(bf16[32,8,1280]{2,1,0:T(8,128)(2,1)S(1)} %bitcast.17), channel_id=1, replica_groups={{0,2,4,6,8,10,12,14,16,18,20,22,24,26,28,30,32,34,36,38,40,42,44,46,48,..., dimensions={0} | all-to-all | bytes 1310720 | tf_op jit(solution)/shard_map/all_to_all | solution.py:395
  136.6 0.0 copy-done.7
  136.6 2.8 %steps.1 = (bf16[4,928]{1,0:T(4,128)(2,1)}, bf16[4,928]{1,0:T(4,128)(2,1)}, bf16[928,480]{1,0:T(8,128)(2,1)}, bf16[928,480]{1,0:T(8,128)(2,1)}) custom-call(bf16[256,1280]{1,0:T(8,128)(2,1)S(1)} %bitcast.16, bf16[256,1280]{1,0:T(8,128)(2,1)S(1)} %bitcast.15, bf16[256,1024]{1,0:T(8,128)(2,1)S(1)} %get-tuple-element.37.tok, ...), custom_call_target="tpu_custom_call" | custom-call | bytes 2374656 | tf_op jit(solution)/shard_map/steps/pallas_call | solution.py:59
  (11 shorter events, 0.1 us)
Async XLA Ops:
  0.6 18.4 %copy-start.4 = (f32[928]{0:T(1024)S(1)}, f32[928]{0:T(1024)}, u32[]{:S(2)}) copy-start(f32[928]{0:T(1024)} %param.16) | copy-start | bytes 11140
  0.6 18.4 %copy-start.3 = (f32[5,928]{1,0:T(8,128)S(1)}, f32[5,928]{1,0:T(8,128)}, u32[]{:S(2)}) copy-start(f32[5,928]{1,0:T(8,128)} %scales_down.1) | copy-start | bytes 55684
  0.7 18.4 %copy-start.2 = (f32[928,5]{0,1:T(8,128)S(1)}, f32[928,5]{0,1:T(8,128)}, u32[]{:S(2)}) copy-start(f32[928,5]{0,1:T(8,128)} %param.13) | copy-start | bytes 55684
  2.3 33.2 %all-to-all-start = ((bf16[32,8,928]{2,1,0:T(8,128)(2,1)}), bf16[32,8,928]{2,1,0:T(8,128)(2,1)S(1)}, u32[]{:S(2)}, u32[]{:S(2)}) async-start(bf16[32,8,928]{2,1,0:T(8,128)(2,1)} %bitcast), calls=%async_computation | async-start | bytes 1048576 | tf_op jit(solution)/shard_map/all_to_all | solution.py:329
  19.0 1.2 copy-start
  20.2 1.2 copy-start.1
  35.4 3.8 %collective-permute-start = (bf16[256,928]{1,0:T(8,128)(2,1)S(1)}, bf16[256,928]{1,0:T(8,128)(2,1)S(1)}, u32[]{:S(2)}, u32[]{:S(2)}) collective-permute-start(bf16[256,928]{1,0:T(8,128)(2,1)S(1)} %bitcast.18), channel_id=1, source_target_pairs={{0,1},{1,0},{2,3},{3,2},{4,5},{5,4},{6,7},{7,6},{8,9},{9,8},{10,11... | collective-permute-start | bytes 1425416 | tf_op jit(solution)/shard_map/ppermute | solution.py:343
  68.2 14.3 %collective-permute-start.1 = (bf16[32,1280]{1,0:T(8,128)(2,1)S(1)}, bf16[32,1280]{1,0:T(8,128)(2,1)S(1)}, u32[]{:S(2)}, u32[]{:S(2)}) collective-permute-start(bf16[32,1280]{1,0:T(8,128)(2,1)S(1)} %convert_element_type.15), channel_id=1, source_target_pairs={{0,64},{64,0},{128,192},{192,128},{256,320},{320,256},{384,448},{4... | collective-permute-start | bytes 245768 | tf_op jit(solution)/shard_map/ppermute | solution.py:366
  82.5 21.0 %copy-start.5 = (f32[480]{0:T(512)S(1)}, f32[480]{0:T(512)}, u32[]{:S(2)}) copy-start(f32[480]{0:T(512)} %param.18) | copy-start | bytes 5764
  105.1 3.9 %collective-permute-start.2 = (bf16[272,1024]{1,0:T(8,128)(2,1)S(1)}, bf16[272,1024]{1,0:T(8,128)(2,1)S(1)}, u32[]{:S(2)}, u32[]{:S(2)}) collective-permute-start(bf16[272,1024]{1,0:T(8,128)(2,1)S(1)} %get-tuple-element.39), channel_id=1, source_target_pairs={{0,1},{1,0},{2,3},{3,2},{4,5},{5,4},{6,7},{7,6},{8,9},{9,8},{10,11... | collective-permute-start | bytes 1671176 | tf_op jit(solution)/shard_map/ppermute | solution.py:385
  109.3 27.2 %copy-start.6 = (f32[928]{0:T(1024)S(1)}, f32[928]{0:T(1024)}, u32[]{:S(2)}) copy-start(f32[928]{0:T(1024)} %param.19) | copy-start | bytes 11140
  109.4 27.2 %copy-start.7 = (f32[480]{0:T(512)S(1)}, f32[480]{0:T(512)}, u32[]{:S(2)}) copy-start(f32[480]{0:T(512)} %param.17) | copy-start | bytes 5764

commit v4 on v3

--- a/solution.py
+++ b/solution.py
@@ -239,6 +239,7 @@
     step_up,
     step_down,
     held,
+    factors,
     sems,
 ):
     width = up_rows.shape[1]
@@ -273,26 +274,45 @@
         ],
         axis=0,
     )
-    columns = jnp.transpose(lines)
+    high = lines.astype(bf16)
+    rest = lines - high.astype(f32)
+    middle = rest.astype(bf16)
+    low = (rest - middle.astype(f32)).astype(bf16)
+    pieces = [jnp.concatenate([p[4 * i : 4 * i + 4] for p in (high, middle, low)], axis=0) for i in (0, 1)]
+    for which in (0, 1):
+        one = (iota((16, WIDTH), 0) % 4 == 0) & (iota((16, WIDTH), 0) < 12)
+        part = jnp.concatenate([pieces[which].astype(f32), jnp.zeros((4, WIDTH), f32)], axis=0)
+        factors[which] = jnp.where(one, part, 0.0).astype(bf16)
     col_new_up = decay_rate * up_columns[...] + keep_rate * squares[0:1, :units] / D
     row_new_down = decay_rate * down_rows[...] + keep_rate * squares[1:2, :units] / D
-    ups = (tok, acts[:, SLOPE:], lax.rsqrt(col_new_up), step_up)
-    downs = (cot, acts[:, :UNITS], lax.rsqrt(row_new_down), step_down)
-    copies = []
-    for first in range(0, width, CHUNK):
-        rows = slice(first, min(first + CHUNK, width))
+    ups = (tok, acts[:, SLOPE:], padded(lax.rsqrt(col_new_up), UNITS), step_up)
+    downs = (cot, acts[:, :UNITS], padded(lax.rsqrt(row_new_down), UNITS), step_down)
+    ones = jnp.ones((16, UNITS), bf16)
+
+    def copy_of(which, first, length, index, out):
+        return pltpu.make_async_copy(
+            held.at[which, pl.ds(first, length)], out.at[pl.ds(first, length)], sems.at[index]
+        )
+
+    def chunk(first, length, index):
+        lanes = pl.ds(first, CHUNK)
         for which, (left, right, scale, out) in enumerate((ups, downs)):
-            grads = mxu(left[:, first : first + CHUNK], right, 0, 0)
-            grads = grads[: rows.stop - first, :units]
-            factor = columns[rows, 4 * which : 4 * which + 1]
-            held[which, rows, :] = (grads * factor * scale).astype(bf16)
-            copy = pltpu.make_async_copy(
-                held.at[which, rows], out.at[rows], sems.at[len(copies)]
-            )
-            copy.start()
-            copies.append(copy)
-    for copy in copies:
-        copy.wait()
+            factor = mxu(factors[which, :, lanes], ones, 0, 0)
+            grads = mxu(left[:, lanes], right, 0, 0) * factor * scale
+            held[which, pl.ds(first, length), :] = grads[:length, :units].astype(bf16)
+            copy_of(which, first, length, 2 * index + which, out).start()
+
+    whole = width // CHUNK
+
+    for index in range(whole):
+        chunk(index * CHUNK, CHUNK, index)
+
+    if width % CHUNK:
+        chunk(whole * CHUNK, width % CHUNK, whole)
+    for index in range(pl.cdiv(width, CHUNK)):
+        first = index * CHUNK
+        for which, out in enumerate((step_up, step_down)):
+            copy_of(which, first, min(CHUNK, width - first), 2 * index + which, out).wait()
 
 
 def on_device(
@@ -406,6 +426,7 @@
         "steps",
         scratch=[
             pltpu.VMEM((2, width, units), bf16),
+            pltpu.VMEM((2, 16, WIDTH), bf16),
             pltpu.SemaphoreType.DMA((2 * pl.cdiv(width, CHUNK),)),
         ],
         out_spaces=[pltpu.VMEM, pltpu.VMEM, pl.ANY, pl.ANY],

time: 140 us -> 140 us (level)
  no operation moved by 1% of the time
where the time goes in v4:
time: 140 us; the launch traced here: 139 us
  blocking collectives  76.1 us (54%)
  starting transfers between devices  32.4 us (23%)
  waiting for transfers between devices  17.1 us (12%)
  Pallas kernels  9.39 us (7%)
  local copies, waits for them, and re-layouts  2.46 us (2%)
    all_to_all x1, blocking collectives, on_device(): lax.all_to_all(parts.reshape(line, -1, LANES), 'wide', 0, 0, axis_index_g...  27.9 us
    all_to_all x1, blocking collectives, on_device(): lax.all_to_all(mixed.reshape(chips, -1, WIDTH + STATS), 'narrow', 0, 0, a...  27.2 us
    all_to_all x1, blocking collectives, on_device(): lax.all_to_all(jnp.broadcast_to(acts[None], (line,) + acts.shape), 'wide'...  21 us
    all_to_all x1, starting transfers between devices, on_device(): lax.all_to_all(copies.reshape(chips, 2 * own, width), 'narrow', 0, 0, axi...  16.7 us
    all_to_all x1, waiting for transfers between devices, on_device(): lax.all_to_all(copies.reshape(chips, 2 * own, width), 'narrow', 0, 0, axi...  12.3 us
    ppermute x1, starting transfers between devices, on_device(): lax.ppermute(sums.astype(bf16), 'wide', half_pairs).astype(f32)  11.9 us
    pallas_call x8, Pallas kernels, call(): pl.pallas_call(kernel, out_shape=[jax.ShapeDtypeStruct(shape, dtype) for...  9.39 us
  transfers between devices with their start and end apart: 4, of which 4 were waited for; matrix products, arithmetic and copies ran while one was open for 0% of the time, Pallas kernels for 2%

profile of v4, /device:TPU:2, one launch (start us, length us, event | category | flops | bytes accessed | tf_op | source)
XLA Modules:
  0.0 139.2 jit_solution(4751710485095977497)
XLA Ops:
  0.6 0.0 copy-start.4
  0.7 0.7 pad_maximum_fusion.1.packed
  1.4 0.9 spread.1
  2.3 16.7 %all-to-all-start = ((bf16[32,8,928]{2,1,0:T(8,128)(2,1)}), bf16[32,8,928]{2,1,0:T(8,128)(2,1)S(1)}, u32[]{:S(2)}, u32[]{:S(2)}) async-start(bf16[32,8,928]{2,1,0:T(8,128)(2,1)} %bitcast), calls=%async_computation | async-start | bytes 1048576 | tf_op jit(solution)/shard_map/all_to_all | solution.py:349
  19.0 0.0 copy-done.4
  19.0 0.0 copy-done.3
  19.0 0.0 copy-done.2
  19.0 0.0 copy-start
  19.0 1.2 copy-done
  20.2 1.2 copy-done.1
  21.4 1.7 %weights.1 = (bf16[1024,512]{1,0:T(8,128)(2,1)S(1)}, bf16[1024,512]{1,0:T(8,128)(2,1)S(1)}, f32[8,512]{1,0:T(8,128)S(1)}) custom-call(bf16[928,480]{1,0:T(8,128)(2,1)S(1)} %copy-done, f32[5,928]{1,0:T(8,128)S(1)} %bitcast.22, bf16[928,480]{1,0:T(8,128)(2,1)S(1)} %bitcast.20, f32[5,928]{1,0:T(8,128)S(1)} %copy-done.3, f32[1,928]{1,0:T(1,128)S(1)} %bitcast.23), custom_call_target="tpu_custom_call" | custom-call | bytes 1822592 | tf_op jit(solution)/shard_map/weights/pallas_call | solution.py:59
  23.1 12.3 %all-to-all-done = bf16[32,8,928]{2,1,0:T(8,128)(2,1)S(1)} async-done(((bf16[32,8,928]{2,1,0:T(8,128)(2,1)}), bf16[32,8,928]{2,1,0:T(8,128)(2,1)S(1)}, u32[]{:S(2)}, u32[]{:S(2)}) %all-to-all-start) | async-done | bytes 475168 | tf_op jit(solution)/shard_map/all_to_all | solution.py:349
  35.4 1.9 %collective-permute-start = (bf16[256,928]{1,0:T(8,128)(2,1)S(1)}, bf16[256,928]{1,0:T(8,128)(2,1)S(1)}, u32[]{:S(2)}, u32[]{:S(2)}) collective-permute-start(bf16[256,928]{1,0:T(8,128)(2,1)S(1)} %bitcast.18), channel_id=1, source_target_pairs={{0,1},{1,0},{2,3},{3,2},{4,5},{5,4},{6,7},{7,6},{8,9},{9,8},{10,11... | collective-permute-start | bytes 1425416 | tf_op jit(solution)/shard_map/ppermute | solution.py:363
  37.3 0.6 own_partial_sums.1
  37.9 1.3 collective-permute-done.other
  39.2 0.9 partial_sums.1
  40.2 27.9 %all_to_all.20 = bf16[8,32,1280]{2,1,0:T(8,128)(2,1)S(1)} all-to-all(bf16[8,32,1280]{2,1,0:T(8,128)(2,1)S(1)} %bitcast.21), channel_id=1, replica_groups={{0,128,256,384,512,640,768,896},{64,192,320,448,576,704,832,960},{1,129..., dimensions={0} | all-to-all | bytes 1310720 | tf_op jit(solution)/shard_map/all_to_all | solution.py:382
  68.0 0.1 convert_reduce_fusion
  68.2 11.9 %collective-permute-start.1 = (bf16[32,1280]{1,0:T(8,128)(2,1)S(1)}, bf16[32,1280]{1,0:T(8,128)(2,1)S(1)}, u32[]{:S(2)}, u32[]{:S(2)}) collective-permute-start(bf16[32,1280]{1,0:T(8,128)(2,1)S(1)} %convert_element_type.15), channel_id=1, source_target_pairs={{0,64},{64,0},{128,192},{192,128},{256,320},{320,256},{384,448},{4... | collective-permute-start | bytes 245768 | tf_op jit(solution)/shard_map/ppermute | solution.py:386
  80.0 2.4 %collective-permute-done.1 = bf16[32,1280]{1,0:T(8,128)(2,1)S(1)} collective-permute-done((bf16[32,1280]{1,0:T(8,128)(2,1)S(1)}, bf16[32,1280]{1,0:T(8,128)(2,1)S(1)}, u32[]{:S(2)}, u32[]{:S(2)}) %collective-permute-start.1) | collective-permute-done | bytes 81952 | tf_op jit(solution)/shard_map/ppermute | solution.py:386
  82.5 0.0 copy-start.5
  82.6 21.0 %all_to_all.21 = bf16[8,32,1280]{2,1,0:T(8,128)(2,1)S(1)} all-to-all(bf16[8,32,1280]{2,1,0:T(8,128)(2,1)S(1)} %broadcast_in_dim.19), channel_id=1, replica_groups={{0,128,256,384,512,640,768,896},{64,192,320,448,576,704,832,960},{1,129..., dimensions={0} | all-to-all | bytes 1310720 | tf_op jit(solution)/shard_map/all_to_all | solution.py:391
  103.5 1.6 %outputs_and_squares.1 = (bf16[272,1024]{1,0:T(8,128)(2,1)S(1)}, f32[8,256]{1,0:T(8,128)S(1)}, f32[2,512]{1,0:T(2,128)S(1)}) custom-call(bf16[256,1280]{1,0:T(8,128)(2,1)S(1)} %bitcast.13, bf16[256,1024]{1,0:T(8,128)(2,1)S(1)} %get-tuple-element.37.tok, bf16[256,1024]{1,0:T(8,128)(2,1)S(1)} %get-tuple-element.38.cot, ...), custom_call_target="tpu_custom_call" | custom-call | flops 939524096 | bytes 3803008 | tf_op jit(solution)/shard_map/outputs_and_squares/pallas_call | solution.py:59
  105.1 1.9 %collective-permute-start.2 = (bf16[272,1024]{1,0:T(8,128)(2,1)S(1)}, bf16[272,1024]{1,0:T(8,128)(2,1)S(1)}, u32[]{:S(2)}, u32[]{:S(2)}) collective-permute-start(bf16[272,1024]{1,0:T(8,128)(2,1)S(1)} %get-tuple-element.39), channel_id=1, source_target_pairs={{0,1},{1,0},{2,3},{3,2},{4,5},{5,4},{6,7},{7,6},{8,9},{9,8},{10,11... | collective-permute-start | bytes 1671176 | tf_op jit(solution)/shard_map/ppermute | solution.py:405
  107.0 0.8 own_outputs.1.keep
  107.9 1.1 collective-permute-done.2.got
  109.0 0.4 pair_sum.1
  109.3 0.0 copy-start.6
  109.4 0.0 copy-start.7
  109.4 27.2 %all_to_all.22 = bf16[32,8,1280]{2,1,0:T(8,128)(2,1)S(1)} all-to-all(bf16[32,8,1280]{2,1,0:T(8,128)(2,1)S(1)} %bitcast.17), channel_id=1, replica_groups={{0,2,4,6,8,10,12,14,16,18,20,22,24,26,28,30,32,34,36,38,40,42,44,46,48,..., dimensions={0} | all-to-all | bytes 1310720 | tf_op jit(solution)/shard_map/all_to_all | solution.py:415
  136.6 0.0 copy-done.7
  136.6 2.6 %steps.1 = (bf16[4,928]{1,0:T(4,128)(2,1)}, bf16[4,928]{1,0:T(4,128)(2,1)}, bf16[928,480]{1,0:T(8,128)(2,1)}, bf16[928,480]{1,0:T(8,128)(2,1)}) custom-call(bf16[256,1280]{1,0:T(8,128)(2,1)S(1)} %bitcast.16, bf16[256,1280]{1,0:T(8,128)(2,1)S(1)} %bitcast.15, bf16[256,1024]{1,0:T(8,128)(2,1)S(1)} %get-tuple-element.37.tok, ...), custom_call_target="tpu_custom_call" | custom-call | bytes 2374656 | tf_op jit(solution)/shard_map/steps/pallas_call | solution.py:59
  (11 shorter events, 0.1 us)
Async XLA Ops:
  0.6 18.4 %copy-start.4 = (f32[928]{0:T(1024)S(1)}, f32[928]{0:T(1024)}, u32[]{:S(2)}) copy-start(f32[928]{0:T(1024)} %param.16) | copy-start | bytes 11140
  0.6 18.4 %copy-start.3 = (f32[5,928]{1,0:T(8,128)S(1)}, f32[5,928]{1,0:T(8,128)}, u32[]{:S(2)}) copy-start(f32[5,928]{1,0:T(8,128)} %scales_down.1) | copy-start | bytes 55684
  0.7 18.4 %copy-start.2 = (f32[928,5]{0,1:T(8,128)S(1)}, f32[928,5]{0,1:T(8,128)}, u32[]{:S(2)}) copy-start(f32[928,5]{0,1:T(8,128)} %param.13) | copy-start | bytes 55684
  2.3 33.2 %all-to-all-start = ((bf16[32,8,928]{2,1,0:T(8,128)(2,1)}), bf16[32,8,928]{2,1,0:T(8,128)(2,1)S(1)}, u32[]{:S(2)}, u32[]{:S(2)}) async-start(bf16[32,8,928]{2,1,0:T(8,128)(2,1)} %bitcast), calls=%async_computation | async-start | bytes 1048576 | tf_op jit(solution)/shard_map/all_to_all | solution.py:349
  19.0 1.2 copy-start
  20.2 1.2 copy-start.1
  35.4 3.8 %collective-permute-start = (bf16[256,928]{1,0:T(8,128)(2,1)S(1)}, bf16[256,928]{1,0:T(8,128)(2,1)S(1)}, u32[]{:S(2)}, u32[]{:S(2)}) collective-permute-start(bf16[256,928]{1,0:T(8,128)(2,1)S(1)} %bitcast.18), channel_id=1, source_target_pairs={{0,1},{1,0},{2,3},{3,2},{4,5},{5,4},{6,7},{7,6},{8,9},{9,8},{10,11... | collective-permute-start | bytes 1425416 | tf_op jit(solution)/shard_map/ppermute | solution.py:363
  68.2 14.3 %collective-permute-start.1 = (bf16[32,1280]{1,0:T(8,128)(2,1)S(1)}, bf16[32,1280]{1,0:T(8,128)(2,1)S(1)}, u32[]{:S(2)}, u32[]{:S(2)}) collective-permute-start(bf16[32,1280]{1,0:T(8,128)(2,1)S(1)} %convert_element_type.15), channel_id=1, source_target_pairs={{0,64},{64,0},{128,192},{192,128},{256,320},{320,256},{384,448},{4... | collective-permute-start | bytes 245768 | tf_op jit(solution)/shard_map/ppermute | solution.py:386
  82.5 21.0 %copy-start.5 = (f32[480]{0:T(512)S(1)}, f32[480]{0:T(512)}, u32[]{:S(2)}) copy-start(f32[480]{0:T(512)} %param.18) | copy-start | bytes 5764
  105.1 3.9 %collective-permute-start.2 = (bf16[272,1024]{1,0:T(8,128)(2,1)S(1)}, bf16[272,1024]{1,0:T(8,128)(2,1)S(1)}, u32[]{:S(2)}, u32[]{:S(2)}) collective-permute-start(bf16[272,1024]{1,0:T(8,128)(2,1)S(1)} %get-tuple-element.39), channel_id=1, source_target_pairs={{0,1},{1,0},{2,3},{3,2},{4,5},{5,4},{6,7},{7,6},{8,9},{9,8},{10,11... | collective-permute-start | bytes 1671176 | tf_op jit(solution)/shard_map/ppermute | solution.py:405
  109.3 27.2 %copy-start.6 = (f32[928]{0:T(1024)S(1)}, f32[928]{0:T(1024)}, u32[]{:S(2)}) copy-start(f32[928]{0:T(1024)} %param.19) | copy-start | bytes 11140
  109.4 27.2 %copy-start.7 = (f32[480]{0:T(512)S(1)}, f32[480]{0:T(512)}, u32[]{:S(2)}) copy-start(f32[480]{0:T(512)} %param.17) | copy-start | bytes 5764

commit v5 on v3

--- a/solution.py
+++ b/solution.py
@@ -62,7 +62,7 @@
             in_specs=[spec] * len(args),
             out_specs=[pl.BlockSpec(memory_space=space) for space in spaces],
             scratch_shapes=list(scratch),
-            compiler_params=pltpu.CompilerParams(vmem_limit_bytes=24 * 1024 * 1024),
+            compiler_params=pltpu.CompilerParams(vmem_limit_bytes=10 * 1024 * 1024),
             cost_estimate=pl.CostEstimate(flops=flops, bytes_accessed=moved, transcendentals=0),
             name=name,
         )(*args)

time: 140 us -> 140 us (level)
  no operation moved by 1% of the time
where the time goes in v5:
time: 140 us; the launch traced here: 139 us
  blocking collectives  76.1 us (54%)
  starting transfers between devices  32.4 us (23%)
  waiting for transfers between devices  17.1 us (12%)
  Pallas kernels  9.6 us (7%)
  local copies, waits for them, and re-layouts  2.46 us (2%)
    all_to_all x1, blocking collectives, on_device(): lax.all_to_all(parts.reshape(line, -1, LANES), 'wide', 0, 0, axis_index_g...  27.9 us
    all_to_all x1, blocking collectives, on_device(): lax.all_to_all(mixed.reshape(chips, -1, WIDTH + STATS), 'narrow', 0, 0, a...  27.2 us
    all_to_all x1, blocking collectives, on_device(): lax.all_to_all(jnp.broadcast_to(acts[None], (line,) + acts.shape), 'wide'...  21 us
    all_to_all x1, starting transfers between devices, on_device(): lax.all_to_all(copies.reshape(chips, 2 * own, width), 'narrow', 0, 0, axi...  16.7 us
    all_to_all x1, waiting for transfers between devices, on_device(): lax.all_to_all(copies.reshape(chips, 2 * own, width), 'narrow', 0, 0, axi...  12.3 us
    ppermute x1, starting transfers between devices, on_device(): lax.ppermute(sums.astype(bf16), 'wide', half_pairs).astype(f32)  11.9 us
    pallas_call x8, Pallas kernels, call(): pl.pallas_call(kernel, out_shape=[jax.ShapeDtypeStruct(shape, dtype) for...  9.6 us
  transfers between devices with their start and end apart: 4, of which 4 were waited for; matrix products, arithmetic and copies ran while one was open for 0% of the time, Pallas kernels for 2%

profile of v5, /device:TPU:2, one launch (start us, length us, event | category | flops | bytes accessed | tf_op | source)
XLA Modules:
  0.0 139.4 jit_solution(10899969500270845649)
XLA Ops:
  0.6 0.0 copy-start.4
  0.7 0.7 pad_maximum_fusion.1.packed
  1.4 0.9 spread.1
  2.3 16.7 %all-to-all-start = ((bf16[32,8,928]{2,1,0:T(8,128)(2,1)}), bf16[32,8,928]{2,1,0:T(8,128)(2,1)S(1)}, u32[]{:S(2)}, u32[]{:S(2)}) async-start(bf16[32,8,928]{2,1,0:T(8,128)(2,1)} %bitcast), calls=%async_computation | async-start | bytes 1048576 | tf_op jit(solution)/shard_map/all_to_all | solution.py:329
  19.0 0.0 copy-done.4
  19.0 0.0 copy-done.3
  19.0 0.0 copy-done.2
  19.0 0.0 copy-start
  19.0 1.2 copy-done
  20.2 1.2 copy-done.1
  21.4 1.7 %weights.1 = (bf16[1024,512]{1,0:T(8,128)(2,1)S(1)}, bf16[1024,512]{1,0:T(8,128)(2,1)S(1)}, f32[8,512]{1,0:T(8,128)S(1)}) custom-call(bf16[928,480]{1,0:T(8,128)(2,1)S(1)} %copy-done, f32[5,928]{1,0:T(8,128)S(1)} %bitcast.22, bf16[928,480]{1,0:T(8,128)(2,1)S(1)} %bitcast.20, f32[5,928]{1,0:T(8,128)S(1)} %copy-done.3, f32[1,928]{1,0:T(1,128)S(1)} %bitcast.23), custom_call_target="tpu_custom_call" | custom-call | bytes 1822592 | tf_op jit(solution)/shard_map/weights/pallas_call | solution.py:59
  23.1 12.3 %all-to-all-done = bf16[32,8,928]{2,1,0:T(8,128)(2,1)S(1)} async-done(((bf16[32,8,928]{2,1,0:T(8,128)(2,1)}), bf16[32,8,928]{2,1,0:T(8,128)(2,1)S(1)}, u32[]{:S(2)}, u32[]{:S(2)}) %all-to-all-start) | async-done | bytes 475168 | tf_op jit(solution)/shard_map/all_to_all | solution.py:329
  35.4 1.9 %collective-permute-start = (bf16[256,928]{1,0:T(8,128)(2,1)S(1)}, bf16[256,928]{1,0:T(8,128)(2,1)S(1)}, u32[]{:S(2)}, u32[]{:S(2)}) collective-permute-start(bf16[256,928]{1,0:T(8,128)(2,1)S(1)} %bitcast.18), channel_id=1, source_target_pairs={{0,1},{1,0},{2,3},{3,2},{4,5},{5,4},{6,7},{7,6},{8,9},{9,8},{10,11... | collective-permute-start | bytes 1425416 | tf_op jit(solution)/shard_map/ppermute | solution.py:343
  37.3 0.6 own_partial_sums.1
  37.9 1.3 collective-permute-done.other
  39.2 0.9 partial_sums.1
  40.2 27.9 %all_to_all.20 = bf16[8,32,1280]{2,1,0:T(8,128)(2,1)S(1)} all-to-all(bf16[8,32,1280]{2,1,0:T(8,128)(2,1)S(1)} %bitcast.21), channel_id=1, replica_groups={{0,128,256,384,512,640,768,896},{64,192,320,448,576,704,832,960},{1,129..., dimensions={0} | all-to-all | bytes 1310720 | tf_op jit(solution)/shard_map/all_to_all | solution.py:362
  68.0 0.1 convert_reduce_fusion
  68.2 11.9 %collective-permute-start.1 = (bf16[32,1280]{1,0:T(8,128)(2,1)S(1)}, bf16[32,1280]{1,0:T(8,128)(2,1)S(1)}, u32[]{:S(2)}, u32[]{:S(2)}) collective-permute-start(bf16[32,1280]{1,0:T(8,128)(2,1)S(1)} %convert_element_type.15), channel_id=1, source_target_pairs={{0,64},{64,0},{128,192},{192,128},{256,320},{320,256},{384,448},{4... | collective-permute-start | bytes 245768 | tf_op jit(solution)/shard_map/ppermute | solution.py:366
  80.0 2.4 %collective-permute-done.1 = bf16[32,1280]{1,0:T(8,128)(2,1)S(1)} collective-permute-done((bf16[32,1280]{1,0:T(8,128)(2,1)S(1)}, bf16[32,1280]{1,0:T(8,128)(2,1)S(1)}, u32[]{:S(2)}, u32[]{:S(2)}) %collective-permute-start.1) | collective-permute-done | bytes 81952 | tf_op jit(solution)/shard_map/ppermute | solution.py:366
  82.5 0.0 copy-start.5
  82.6 21.0 %all_to_all.21 = bf16[8,32,1280]{2,1,0:T(8,128)(2,1)S(1)} all-to-all(bf16[8,32,1280]{2,1,0:T(8,128)(2,1)S(1)} %broadcast_in_dim.19), channel_id=1, replica_groups={{0,128,256,384,512,640,768,896},{64,192,320,448,576,704,832,960},{1,129..., dimensions={0} | all-to-all | bytes 1310720 | tf_op jit(solution)/shard_map/all_to_all | solution.py:371
  103.5 1.6 %outputs_and_squares.1 = (bf16[272,1024]{1,0:T(8,128)(2,1)S(1)}, f32[8,256]{1,0:T(8,128)S(1)}, f32[2,512]{1,0:T(2,128)S(1)}) custom-call(bf16[256,1280]{1,0:T(8,128)(2,1)S(1)} %bitcast.13, bf16[256,1024]{1,0:T(8,128)(2,1)S(1)} %get-tuple-element.37.tok, bf16[256,1024]{1,0:T(8,128)(2,1)S(1)} %get-tuple-element.38.cot, ...), custom_call_target="tpu_custom_call" | custom-call | flops 939524096 | bytes 3803008 | tf_op jit(solution)/shard_map/outputs_and_squares/pallas_call | solution.py:59
  105.1 1.9 %collective-permute-start.2 = (bf16[272,1024]{1,0:T(8,128)(2,1)S(1)}, bf16[272,1024]{1,0:T(8,128)(2,1)S(1)}, u32[]{:S(2)}, u32[]{:S(2)}) collective-permute-start(bf16[272,1024]{1,0:T(8,128)(2,1)S(1)} %get-tuple-element.39), channel_id=1, source_target_pairs={{0,1},{1,0},{2,3},{3,2},{4,5},{5,4},{6,7},{7,6},{8,9},{9,8},{10,11... | collective-permute-start | bytes 1671176 | tf_op jit(solution)/shard_map/ppermute | solution.py:385
  107.0 0.8 own_outputs.1.keep
  107.9 1.1 collective-permute-done.2.got
  109.0 0.4 pair_sum.1
  109.3 0.0 copy-start.6
  109.4 0.0 copy-start.7
  109.4 27.2 %all_to_all.22 = bf16[32,8,1280]{2,1,0:T(8,128)(2,1)S(1)} all-to-all(bf16[32,8,1280]{2,1,0:T(8,128)(2,1)S(1)} %bitcast.17), channel_id=1, replica_groups={{0,2,4,6,8,10,12,14,16,18,20,22,24,26,28,30,32,34,36,38,40,42,44,46,48,..., dimensions={0} | all-to-all | bytes 1310720 | tf_op jit(solution)/shard_map/all_to_all | solution.py:395
  136.6 0.0 copy-done.7
  136.6 2.8 %steps.1 = (bf16[4,928]{1,0:T(4,128)(2,1)}, bf16[4,928]{1,0:T(4,128)(2,1)}, bf16[928,480]{1,0:T(8,128)(2,1)}, bf16[928,480]{1,0:T(8,128)(2,1)}) custom-call(bf16[256,1280]{1,0:T(8,128)(2,1)S(1)} %bitcast.16, bf16[256,1280]{1,0:T(8,128)(2,1)S(1)} %bitcast.15, bf16[256,1024]{1,0:T(8,128)(2,1)S(1)} %get-tuple-element.37.tok, ...), custom_call_target="tpu_custom_call" | custom-call | bytes 2374656 | tf_op jit(solution)/shard_map/steps/pallas_call | solution.py:59
  (11 shorter events, 0.1 us)
Async XLA Ops:
  0.6 18.4 %copy-start.4 = (f32[928]{0:T(1024)S(1)}, f32[928]{0:T(1024)}, u32[]{:S(2)}) copy-start(f32[928]{0:T(1024)} %param.16) | copy-start | bytes 11140
  0.6 18.4 %copy-start.3 = (f32[5,928]{1,0:T(8,128)S(1)}, f32[5,928]{1,0:T(8,128)}, u32[]{:S(2)}) copy-start(f32[5,928]{1,0:T(8,128)} %scales_down.1) | copy-start | bytes 55684
  0.7 18.4 %copy-start.2 = (f32[928,5]{0,1:T(8,128)S(1)}, f32[928,5]{0,1:T(8,128)}, u32[]{:S(2)}) copy-start(f32[928,5]{0,1:T(8,128)} %param.13) | copy-start | bytes 55684
  2.3 33.2 %all-to-all-start = ((bf16[32,8,928]{2,1,0:T(8,128)(2,1)}), bf16[32,8,928]{2,1,0:T(8,128)(2,1)S(1)}, u32[]{:S(2)}, u32[]{:S(2)}) async-start(bf16[32,8,928]{2,1,0:T(8,128)(2,1)} %bitcast), calls=%async_computation | async-start | bytes 1048576 | tf_op jit(solution)/shard_map/all_to_all | solution.py:329
  19.0 1.2 copy-start
  20.2 1.2 copy-start.1
  35.4 3.8 %collective-permute-start = (bf16[256,928]{1,0:T(8,128)(2,1)S(1)}, bf16[256,928]{1,0:T(8,128)(2,1)S(1)}, u32[]{:S(2)}, u32[]{:S(2)}) collective-permute-start(bf16[256,928]{1,0:T(8,128)(2,1)S(1)} %bitcast.18), channel_id=1, source_target_pairs={{0,1},{1,0},{2,3},{3,2},{4,5},{5,4},{6,7},{7,6},{8,9},{9,8},{10,11... | collective-permute-start | bytes 1425416 | tf_op jit(solution)/shard_map/ppermute | solution.py:343
  68.2 14.3 %collective-permute-start.1 = (bf16[32,1280]{1,0:T(8,128)(2,1)S(1)}, bf16[32,1280]{1,0:T(8,128)(2,1)S(1)}, u32[]{:S(2)}, u32[]{:S(2)}) collective-permute-start(bf16[32,1280]{1,0:T(8,128)(2,1)S(1)} %convert_element_type.15), channel_id=1, source_target_pairs={{0,64},{64,0},{128,192},{192,128},{256,320},{320,256},{384,448},{4... | collective-permute-start | bytes 245768 | tf_op jit(solution)/shard_map/ppermute | solution.py:366
  82.5 21.0 %copy-start.5 = (f32[480]{0:T(512)S(1)}, f32[480]{0:T(512)}, u32[]{:S(2)}) copy-start(f32[480]{0:T(512)} %param.18) | copy-start | bytes 5764
  105.1 3.9 %collective-permute-start.2 = (bf16[272,1024]{1,0:T(8,128)(2,1)S(1)}, bf16[272,1024]{1,0:T(8,128)(2,1)S(1)}, u32[]{:S(2)}, u32[]{:S(2)}) collective-permute-start(bf16[272,1024]{1,0:T(8,128)(2,1)S(1)} %get-tuple-element.39), channel_id=1, source_target_pairs={{0,1},{1,0},{2,3},{3,2},{4,5},{5,4},{6,7},{7,6},{8,9},{9,8},{10,11... | collective-permute-start | bytes 1671176 | tf_op jit(solution)/shard_map/ppermute | solution.py:385
  109.3 27.2 %copy-start.6 = (f32[928]{0:T(1024)S(1)}, f32[928]{0:T(1024)}, u32[]{:S(2)}) copy-start(f32[928]{0:T(1024)} %param.19) | copy-start | bytes 11140
  109.4 27.2 %copy-start.7 = (f32[480]{0:T(512)S(1)}, f32[480]{0:T(512)}, u32[]{:S(2)}) copy-start(f32[480]{0:T(512)} %param.17) | copy-start | bytes 5764
